TPU v7x, 32 devices: a whole 2x2x4 slice. The times are simulated.
32 devices in a mesh: band: 4 (over z), ty: 4 (over y, core), tx: 2 (over x).
Axes of the slice: x: 2, y: 2, z: 4, core: 2. Of those that a mesh axis runs over, the one named last changes fastest.
Arguments:
- dirty: float32 [8, 1024, 512], P('band', 'ty', 'tx'), may hold values from -6 to 6
- psf: bfloat16 [8, 20, 2304], P('band'), may hold values from -4 to 4
- comp_tile: int32 [1024, 1], P(('ty', 'tx')), may hold values from 0 to 7; in each aligned block of 128 rows (0 to 127, 128 to 255, ...) at most 32 rows name the same one
- comp_offset: int32 [1024, 2], P(('ty', 'tx')), may hold values from 0 to 255
- comp_scale: int32 [1024], P(('ty', 'tx')), may hold values from 0 to 4
- comp_amp: float32 [1024, 4], P(('ty', 'tx')), may hold values from -6 to 6
- fit_weight: float32 [8, 4], P('band'), may hold values from -5 to 5
Outputs:
- residual: float32 [8, 1024, 512], P('band', 'ty', 'tx')
- taylor_fit: float32 [4, 1024, 512], P('band', 'ty', 'tx')
Inputs may be any that keep to these rules, and one draw needn't show every extreme that they name: `comp_tile`: the 128 components of one device name at most 32 components for one tile, and exactly 32 for some tile on some device.
All inputs are finite; a program needn't handle non-finite values.
Results may differ from a plain program's by a relative error of at most 0.0022.
Values may be sent and summed in bfloat16 or wider, within the bound.
No kernel may reach another device: no remote copies, remote signals or barrier semaphores. Data moves between devices by JAX's collectives and lax.ppermute only.
A program may use at most 64 MiB of HBM per device.

v0:
```python
import jax
import jax.numpy as jnp
from jax import lax
from jax.sharding import PartitionSpec as P

TAYLOR = 4
SCALES = 5
PATCH = 48


def passed_along(value, axis, steps):
    count = lax.axis_size(axis)
    initial, last = (max(0, -steps), min(count, count - steps))
    return lax.ppermute(value, axis, [(source, source + steps) for source in range(initial, last)])


def make_patches(amps, scales, psf_local):
    count = amps.shape[0]
    select = (scales[:, None] == jnp.arange(SCALES, dtype=jnp.int32)[None, :]).astype(jnp.float32)
    coef = (amps[:, :, None] * select[:, None, :]).reshape(count, TAYLOR * SCALES)
    built = jnp.einsum(
        "sk,bkp->sbp", coef, psf_local.astype(jnp.float32), precision=lax.Precision.HIGHEST
    )
    return built.astype(jnp.bfloat16)


def pick_rows(onehot, values):
    return jnp.sum(
        jnp.where(onehot[:, :, None], values[None, :, :], jnp.zeros((), values.dtype)), axis=1
    )


def render(getter, slots, bands_here, height, width):
    block = 16
    span = jnp.arange(PATCH, dtype=jnp.int32)
    row_ids = jnp.arange(height, dtype=jnp.int32)
    col_ids = jnp.arange(width, dtype=jnp.int32)

    def step(index, model):
        patch_blk, offs_blk = getter(index * block)
        patch_four = patch_blk.reshape(block, bands_here, PATCH, PATCH)
        col_table = (
            col_ids[None, None, :] == offs_blk[:, 1][:, None, None] + span[None, :, None]
        ).astype(jnp.bfloat16)
        placed = jnp.einsum(
            "cbuv,cvw->bcuw", patch_four, col_table, preferred_element_type=jnp.float32
        ).astype(jnp.bfloat16)
        row_table = (
            row_ids[:, None, None] == offs_blk[:, 0][None, :, None] + span[None, None, :]
        ).astype(jnp.bfloat16)
        row_table = row_table.reshape(height, block * PATCH)
        placed = placed.reshape(bands_here, block * PATCH, width)
        return model + jnp.einsum(
            "hk,bkw->bhw", row_table, placed, preferred_element_type=jnp.float32
        )

    start = jnp.zeros((bands_here, height, width), jnp.float32)
    return lax.fori_loop(0, slots // block, step, start)


def per_device(dirty, psf, comp_tile, comp_offset, comp_scale, comp_amp, fit_weight):
    bands_here = dirty.shape[0]
    tile_side = dirty.shape[1]
    height = tile_side + PATCH
    n_tiles = lax.axis_size("ty") * lax.axis_size("tx")
    listed = comp_tile.shape[0]
    cap_each = max(2, 2 * listed // n_tiles)
    slots = n_tiles * cap_each
    dest = comp_tile[:, 0]
    order = jnp.arange(listed, dtype=jnp.int32)
    same = (dest[:, None] == dest[None, :]) & (order[:, None] > order[None, :])
    rank = jnp.sum(same.astype(jnp.int32), axis=1)
    slot_of = dest * cap_each + rank
    onehot = jnp.arange(slots, dtype=jnp.int32)[:, None] == slot_of[None, :]
    offs_send = pick_rows(onehot, comp_offset)
    packed = jnp.concatenate([offs_send, pick_rows(onehot, comp_scale[:, None])], axis=1)
    amps_send = pick_rows(onehot, comp_amp)
    amps_got, ints_got = (
        lax.all_to_all(amps_send, ("ty", "tx"), split_axis=0, concat_axis=0, tiled=True),
        lax.all_to_all(packed, ("ty", "tx"), split_axis=0, concat_axis=0, tiled=True),
    )

    def getter(first):
        amps_blk = lax.dynamic_slice_in_dim(amps_got, first, 16, 0)
        ints_blk = lax.dynamic_slice_in_dim(ints_got, first, 16, 0)
        return (make_patches(amps_blk, ints_blk[:, 2], psf), ints_blk[:, 0:2])

    model = render(getter, slots, bands_here, height, height)
    right_strip = model[:, :, tile_side:].reshape(bands_here, -1)
    came_right = passed_along(right_strip, "tx", 1)
    model = model.at[:, :, :PATCH].add(came_right.reshape(bands_here, height, PATCH))
    model = model[:, :, :tile_side]
    lower_strip = model[:, tile_side:, :].reshape(bands_here, -1)
    came_lower = passed_along(lower_strip, "ty", 1)
    model = model.at[:, :PATCH, :].add(came_lower.reshape(bands_here, PATCH, tile_side))
    residual = dirty - model[:, :tile_side, :]
    taylor_fit = lax.psum_scatter(
        jnp.einsum("bt,byx->tyx", fit_weight, residual, precision=lax.Precision.HIGHEST),
        "band",
        scatter_dimension=0,
        tiled=True,
    )
    return (residual, taylor_fit)


def solution(mesh):
    return jax.shard_map(
        per_device,
        mesh=mesh,
        in_specs=(
            P("band", "ty", "tx"),
            P("band", None, None),
            P(("ty", "tx"), None),
            P(("ty", "tx"), None),
            P(("ty", "tx")),
            P(("ty", "tx"), None),
            P("band", None),
        ),
        out_specs=(P("band", "ty", "tx"), P("band", "ty", "tx")),
        check_vma=False,
    )
```

profile of v0, /device:TPU:0, one launch (start us, length us, event | category | flops | bytes accessed | tf_op | source)
XLA Modules:
  0.0 121.4 jit_solution(7272169568697328382)
XLA Ops:
  7.2 0.9 convert_reduce_fusion
  11.2 5.2 %all-to-all-start = ((s32[8,32,3]{1,2,0:T(4,128)}), s32[8,32,3]{1,2,0:T(4,128)S(1)}, u32[]{:S(2)}, u32[]{:S(2)}) async-start(s32[8,32,3]{1,2,0:T(4,128)} %copy.48), calls=%async_computation | async-start | bytes 32768 | tf_op jit(solution)/shard_map/all_to_all | solution.py:80
  16.3 0.9 select_reduce_fusion
  18.0 3.0 %all-to-all-done = s32[8,32,3]{1,2,0:T(4,128)S(1)} async-done(((s32[8,32,3]{1,2,0:T(4,128)}), s32[8,32,3]{1,2,0:T(4,128)S(1)}, u32[]{:S(2)}, u32[]{:S(2)}) %all-to-all-start) | async-done | bytes 3104 | tf_op jit(solution)/shard_map/all_to_all | solution.py:80
  21.1 3.3 %all-to-all-start.1 = ((f32[8,1,128]{2,1,0:T(1,128)}), f32[8,1,128]{2,1,0:T(1,128)S(1)}, u32[]{:S(2)}, u32[]{:S(2)}) async-start(f32[8,1,128]{2,1,0:T(1,128)} %reshape.305), calls=%async_computation.1 | async-start | bytes 8192 | tf_op jit(solution)/shard_map/all_to_all | solution.py:79
  24.4 0.9 copy.52
  25.5 3.4 %all-to-all-done.1 = f32[8,1,128]{2,1,0:T(1,128)S(1)} async-done(((f32[8,1,128]{2,1,0:T(1,128)}), f32[8,1,128]{2,1,0:T(1,128)S(1)}, u32[]{:S(2)}, u32[]{:S(2)}) %all-to-all-start.1) | async-done | bytes 4128 | tf_op jit(solution)/shard_map/all_to_all | solution.py:79
  30.2 39.3 %while.18 = (s32[]{:T(128)}, f32[2,304,304]{1,2,0:T(8,128)S(1)}, s32[256,3]{0,1:T(4,128)S(1)}, f32[256,4]{0,1:T(4,128)S(1)}, bf16[2,20,2304]{2,1,0:T(8,128)(2,1)...) while((s32[]{:T(128)}, f32[2,304,304]{1,2,0:T(8,128)S(1)}, ...), condition=%wide.region_5.6_spmd.clone.clone, body=%wide.region_4.5_spmd.clone.clone.sunk | while | flops 347802592 | bytes 2272741 | solution.py:58
  31.4 1.3 %fusion.37 = f32[2,304,304]{1,2,0:T(8,128)S(1)} fusion(bf16[16,2,48,48]{3,2,0,1:T(8,128)(2,1)S(1)} %reshape.308, f32[2,304,304]{1,2,0:T(8,128)S(1)} %get-tuple-element.317, s32[16,48]{1,0:T(8,128)S(1)} %get-tuple-element.305, s32[16,48]{1,0:T(8,128)S(1)} %get-tuple-element.306, pred[]{:T(512)S(6)} %compare.15), kind=kOutput, calls=%fused_computation.7.clone.1 | convolution fusion | flops 330032128 | bytes 1632257 | tf_op jit(solution)/shard_map/while/body/eval_jaxpr/hk,bkw->bhw/dot_general | solution.py:53
  33.8 1.3 %fusion.37 = f32[2,304,304]{1,2,0:T(8,128)S(1)} fusion(bf16[16,2,48,48]{3,2,0,1:T(8,128)(2,1)S(1)} %reshape.308, f32[2,304,304]{1,2,0:T(8,128)S(1)} %get-tuple-element.317, s32[16,48]{1,0:T(8,128)S(1)} %get-tuple-element.305, s32[16,48]{1,0:T(8,128)S(1)} %get-tuple-element.306, pred[]{:T(512)S(6)} %compare.15), kind=kOutput, calls=%fused_computation.7.clone.1 | convolution fusion | flops 330032128 | bytes 1632257 | tf_op jit(solution)/shard_map/while/body/eval_jaxpr/hk,bkw->bhw/dot_general | solution.py:53
  36.3 1.3 %fusion.37 = f32[2,304,304]{1,2,0:T(8,128)S(1)} fusion(bf16[16,2,48,48]{3,2,0,1:T(8,128)(2,1)S(1)} %reshape.308, f32[2,304,304]{1,2,0:T(8,128)S(1)} %get-tuple-element.317, s32[16,48]{1,0:T(8,128)S(1)} %get-tuple-element.305, s32[16,48]{1,0:T(8,128)S(1)} %get-tuple-element.306, pred[]{:T(512)S(6)} %compare.15), kind=kOutput, calls=%fused_computation.7.clone.1 | convolution fusion | flops 330032128 | bytes 1632257 | tf_op jit(solution)/shard_map/while/body/eval_jaxpr/hk,bkw->bhw/dot_general | solution.py:53
  38.7 1.3 %fusion.37 = f32[2,304,304]{1,2,0:T(8,128)S(1)} fusion(bf16[16,2,48,48]{3,2,0,1:T(8,128)(2,1)S(1)} %reshape.308, f32[2,304,304]{1,2,0:T(8,128)S(1)} %get-tuple-element.317, s32[16,48]{1,0:T(8,128)S(1)} %get-tuple-element.305, s32[16,48]{1,0:T(8,128)S(1)} %get-tuple-element.306, pred[]{:T(512)S(6)} %compare.15), kind=kOutput, calls=%fused_computation.7.clone.1 | convolution fusion | flops 330032128 | bytes 1632257 | tf_op jit(solution)/shard_map/while/body/eval_jaxpr/hk,bkw->bhw/dot_general | solution.py:53
  41.2 1.3 %fusion.37 = f32[2,304,304]{1,2,0:T(8,128)S(1)} fusion(bf16[16,2,48,48]{3,2,0,1:T(8,128)(2,1)S(1)} %reshape.308, f32[2,304,304]{1,2,0:T(8,128)S(1)} %get-tuple-element.317, s32[16,48]{1,0:T(8,128)S(1)} %get-tuple-element.305, s32[16,48]{1,0:T(8,128)S(1)} %get-tuple-element.306, pred[]{:T(512)S(6)} %compare.15), kind=kOutput, calls=%fused_computation.7.clone.1 | convolution fusion | flops 330032128 | bytes 1632257 | tf_op jit(solution)/shard_map/while/body/eval_jaxpr/hk,bkw->bhw/dot_general | solution.py:53
  43.6 1.3 %fusion.37 = f32[2,304,304]{1,2,0:T(8,128)S(1)} fusion(bf16[16,2,48,48]{3,2,0,1:T(8,128)(2,1)S(1)} %reshape.308, f32[2,304,304]{1,2,0:T(8,128)S(1)} %get-tuple-element.317, s32[16,48]{1,0:T(8,128)S(1)} %get-tuple-element.305, s32[16,48]{1,0:T(8,128)S(1)} %get-tuple-element.306, pred[]{:T(512)S(6)} %compare.15), kind=kOutput, calls=%fused_computation.7.clone.1 | convolution fusion | flops 330032128 | bytes 1632257 | tf_op jit(solution)/shard_map/while/body/eval_jaxpr/hk,bkw->bhw/dot_general | solution.py:53
  46.1 1.3 %fusion.37 = f32[2,304,304]{1,2,0:T(8,128)S(1)} fusion(bf16[16,2,48,48]{3,2,0,1:T(8,128)(2,1)S(1)} %reshape.308, f32[2,304,304]{1,2,0:T(8,128)S(1)} %get-tuple-element.317, s32[16,48]{1,0:T(8,128)S(1)} %get-tuple-element.305, s32[16,48]{1,0:T(8,128)S(1)} %get-tuple-element.306, pred[]{:T(512)S(6)} %compare.15), kind=kOutput, calls=%fused_computation.7.clone.1 | convolution fusion | flops 330032128 | bytes 1632257 | tf_op jit(solution)/shard_map/while/body/eval_jaxpr/hk,bkw->bhw/dot_general | solution.py:53
  48.5 1.3 %fusion.37 = f32[2,304,304]{1,2,0:T(8,128)S(1)} fusion(bf16[16,2,48,48]{3,2,0,1:T(8,128)(2,1)S(1)} %reshape.308, f32[2,304,304]{1,2,0:T(8,128)S(1)} %get-tuple-element.317, s32[16,48]{1,0:T(8,128)S(1)} %get-tuple-element.305, s32[16,48]{1,0:T(8,128)S(1)} %get-tuple-element.306, pred[]{:T(512)S(6)} %compare.15), kind=kOutput, calls=%fused_computation.7.clone.1 | convolution fusion | flops 330032128 | bytes 1632257 | tf_op jit(solution)/shard_map/while/body/eval_jaxpr/hk,bkw->bhw/dot_general | solution.py:53
  51.0 1.3 %fusion.37 = f32[2,304,304]{1,2,0:T(8,128)S(1)} fusion(bf16[16,2,48,48]{3,2,0,1:T(8,128)(2,1)S(1)} %reshape.308, f32[2,304,304]{1,2,0:T(8,128)S(1)} %get-tuple-element.317, s32[16,48]{1,0:T(8,128)S(1)} %get-tuple-element.305, s32[16,48]{1,0:T(8,128)S(1)} %get-tuple-element.306, pred[]{:T(512)S(6)} %compare.15), kind=kOutput, calls=%fused_computation.7.clone.1 | convolution fusion | flops 330032128 | bytes 1632257 | tf_op jit(solution)/shard_map/while/body/eval_jaxpr/hk,bkw->bhw/dot_general | solution.py:53
  53.5 1.3 %fusion.37 = f32[2,304,304]{1,2,0:T(8,128)S(1)} fusion(bf16[16,2,48,48]{3,2,0,1:T(8,128)(2,1)S(1)} %reshape.308, f32[2,304,304]{1,2,0:T(8,128)S(1)} %get-tuple-element.317, s32[16,48]{1,0:T(8,128)S(1)} %get-tuple-element.305, s32[16,48]{1,0:T(8,128)S(1)} %get-tuple-element.306, pred[]{:T(512)S(6)} %compare.15), kind=kOutput, calls=%fused_computation.7.clone.1 | convolution fusion | flops 330032128 | bytes 1632257 | tf_op jit(solution)/shard_map/while/body/eval_jaxpr/hk,bkw->bhw/dot_general | solution.py:53
  55.9 1.3 %fusion.37 = f32[2,304,304]{1,2,0:T(8,128)S(1)} fusion(bf16[16,2,48,48]{3,2,0,1:T(8,128)(2,1)S(1)} %reshape.308, f32[2,304,304]{1,2,0:T(8,128)S(1)} %get-tuple-element.317, s32[16,48]{1,0:T(8,128)S(1)} %get-tuple-element.305, s32[16,48]{1,0:T(8,128)S(1)} %get-tuple-element.306, pred[]{:T(512)S(6)} %compare.15), kind=kOutput, calls=%fused_computation.7.clone.1 | convolution fusion | flops 330032128 | bytes 1632257 | tf_op jit(solution)/shard_map/while/body/eval_jaxpr/hk,bkw->bhw/dot_general | solution.py:53
  58.4 1.3 %fusion.37 = f32[2,304,304]{1,2,0:T(8,128)S(1)} fusion(bf16[16,2,48,48]{3,2,0,1:T(8,128)(2,1)S(1)} %reshape.308, f32[2,304,304]{1,2,0:T(8,128)S(1)} %get-tuple-element.317, s32[16,48]{1,0:T(8,128)S(1)} %get-tuple-element.305, s32[16,48]{1,0:T(8,128)S(1)} %get-tuple-element.306, pred[]{:T(512)S(6)} %compare.15), kind=kOutput, calls=%fused_computation.7.clone.1 | convolution fusion | flops 330032128 | bytes 1632257 | tf_op jit(solution)/shard_map/while/body/eval_jaxpr/hk,bkw->bhw/dot_general | solution.py:53
  60.8 1.3 %fusion.37 = f32[2,304,304]{1,2,0:T(8,128)S(1)} fusion(bf16[16,2,48,48]{3,2,0,1:T(8,128)(2,1)S(1)} %reshape.308, f32[2,304,304]{1,2,0:T(8,128)S(1)} %get-tuple-element.317, s32[16,48]{1,0:T(8,128)S(1)} %get-tuple-element.305, s32[16,48]{1,0:T(8,128)S(1)} %get-tuple-element.306, pred[]{:T(512)S(6)} %compare.15), kind=kOutput, calls=%fused_computation.7.clone.1 | convolution fusion | flops 330032128 | bytes 1632257 | tf_op jit(solution)/shard_map/while/body/eval_jaxpr/hk,bkw->bhw/dot_general | solution.py:53
  63.3 1.3 %fusion.37 = f32[2,304,304]{1,2,0:T(8,128)S(1)} fusion(bf16[16,2,48,48]{3,2,0,1:T(8,128)(2,1)S(1)} %reshape.308, f32[2,304,304]{1,2,0:T(8,128)S(1)} %get-tuple-element.317, s32[16,48]{1,0:T(8,128)S(1)} %get-tuple-element.305, s32[16,48]{1,0:T(8,128)S(1)} %get-tuple-element.306, pred[]{:T(512)S(6)} %compare.15), kind=kOutput, calls=%fused_computation.7.clone.1 | convolution fusion | flops 330032128 | bytes 1632257 | tf_op jit(solution)/shard_map/while/body/eval_jaxpr/hk,bkw->bhw/dot_general | solution.py:53
  65.7 1.3 %fusion.37 = f32[2,304,304]{1,2,0:T(8,128)S(1)} fusion(bf16[16,2,48,48]{3,2,0,1:T(8,128)(2,1)S(1)} %reshape.308, f32[2,304,304]{1,2,0:T(8,128)S(1)} %get-tuple-element.317, s32[16,48]{1,0:T(8,128)S(1)} %get-tuple-element.305, s32[16,48]{1,0:T(8,128)S(1)} %get-tuple-element.306, pred[]{:T(512)S(6)} %compare.15), kind=kOutput, calls=%fused_computation.7.clone.1 | convolution fusion | flops 330032128 | bytes 1632257 | tf_op jit(solution)/shard_map/while/body/eval_jaxpr/hk,bkw->bhw/dot_general | solution.py:53
  68.2 1.3 %fusion.37 = f32[2,304,304]{1,2,0:T(8,128)S(1)} fusion(bf16[16,2,48,48]{3,2,0,1:T(8,128)(2,1)S(1)} %reshape.308, f32[2,304,304]{1,2,0:T(8,128)S(1)} %get-tuple-element.317, s32[16,48]{1,0:T(8,128)S(1)} %get-tuple-element.305, s32[16,48]{1,0:T(8,128)S(1)} %get-tuple-element.306, pred[]{:T(512)S(6)} %compare.15), kind=kOutput, calls=%fused_computation.7.clone.1 | convolution fusion | flops 330032128 | bytes 1632257 | tf_op jit(solution)/shard_map/while/body/eval_jaxpr/hk,bkw->bhw/dot_general | solution.py:53
  69.9 2.5 %collective-permute-start = (f32[2,14592]{1,0:T(2,128)S(1)}, f32[2,14592]{1,0:T(2,128)S(1)}, u32[]{:S(2)}, u32[]{:S(2)}) collective-permute-start(f32[2,14592]{1,0:T(2,128)S(1)} %reshape.294), channel_id=1, source_target_pairs={{0,1},{2,3},{4,5},{6,7},{8,9},{10,11},{12,13},{14,15},{16,17},{18,... | collective-permute-start | bytes 350216 | tf_op jit(solution)/shard_map/ppermute | solution.py:14
  72.7 2.0 %collective-permute-done = f32[2,14592]{1,0:T(2,128)S(1)} collective-permute-done((f32[2,14592]{1,0:T(2,128)S(1)}, f32[2,14592]{1,0:T(2,128)S(1)}, u32[]{:S(2)}, u32[]{:S(2)}) %collective-permute-start) | collective-permute-done | bytes 116768 | tf_op jit(solution)/shard_map/ppermute | solution.py:14
  75.0 1.3 %scatter-add.6 = f32[2,304,304]{2,1,0:T(8,128)S(1)} dynamic-update-slice(f32[2,304,304]{2,1,0:T(8,128)S(1)} %copy.55, f32[2,304,48]{2,1,0:T(8,128)S(1)} %slice_add_fusion, s32[]{:T(128)} %constant.88.clone.1, s32[]{:T(128)} %constant.88.clone.1, s32[]{:T(128)} %constant.88.clone.1) | dynamic-update-slice | bytes 233476 | tf_op jit(solution)/shard_map/scatter-add | solution.py:91
  76.5 1.4 %collective-permute-start.1 = (f32[2,12288]{1,0:T(2,128)S(1)}, f32[2,12288]{1,0:T(2,128)S(1)}, u32[]{:S(2)}, u32[]{:S(2)}) collective-permute-start(f32[2,12288]{1,0:T(2,128)S(1)} %bitcast.80), channel_id=1, source_target_pairs={{0,2},{2,4},{4,6},{1,3},{3,5},{5,7},{8,10},{10,12},{12,14},{9,11},... | collective-permute-start | bytes 294920 | tf_op jit(solution)/shard_map/ppermute | solution.py:14
  77.9 0.9 collective-permute-done.1
  78.9 2.1 %convolution_bitcast_fusion = f32[4,256,256]{2,0,1:T(4,128)S(1)} fusion(f32[2,256,256]{2,1,0:T(8,128)S(1)} %slice_subtract_fusion, f32[2,4]{1,0:T(2,128)S(1)} %copy-done), kind=kOutput, calls=%fused_computation.25 | convolution fusion | flops 6291456 | bytes 1572896 | tf_op jit(solution)/shard_map/bt,byx->tyx/dot_general | solution.py:98
  81.0 1.2 copy.57
  82.3 32.3 %reduce-scatter.2.cloned.1.call-done = f32[1,256,256]{2,1,0:T(8,128)} async-done(((f32[4,256,256]{2,1,0:T(8,128)}), f32[1,256,256]{2,1,0:T(8,128)}) %reduce-scatter.2.cloned.1.call-update) | async-done | bytes 262160 | tf_op jit(solution)/shard_map/reduce_scatter | solution.py:97
  (182 shorter events, 24.6 us)
Async XLA Ops:
  7.2 71.8 %copy-start = (f32[2,4]{1,0:T(2,128)S(1)}, f32[2,4]{1,0:T(2,128)}, u32[]{:S(2)}) copy-start(f32[2,4]{1,0:T(2,128)} %param.19) | copy-start | bytes 100
  11.2 9.9 %all-to-all-start = ((s32[8,32,3]{1,2,0:T(4,128)}), s32[8,32,3]{1,2,0:T(4,128)S(1)}, u32[]{:S(2)}, u32[]{:S(2)}) async-start(s32[8,32,3]{1,2,0:T(4,128)} %copy.48), calls=%async_computation | async-start | bytes 32768 | tf_op jit(solution)/shard_map/all_to_all | solution.py:80
  21.1 7.8 %all-to-all-start.1 = ((f32[8,1,128]{2,1,0:T(1,128)}), f32[8,1,128]{2,1,0:T(1,128)S(1)}, u32[]{:S(2)}, u32[]{:S(2)}) async-start(f32[8,1,128]{2,1,0:T(1,128)} %reshape.305), calls=%async_computation.1 | async-start | bytes 8192 | tf_op jit(solution)/shard_map/all_to_all | solution.py:79
  24.4 90.2 %reduce-scatter.2.cloned.1.call-start = ((), (), s32[]{:S(2)}) async-start(), calls=%async_computation.3 | async-start | bytes 1310720 | tf_op jit(solution)/shard_map/reduce_scatter | solution.py:97
  69.9 4.9 %collective-permute-start = (f32[2,14592]{1,0:T(2,128)S(1)}, f32[2,14592]{1,0:T(2,128)S(1)}, u32[]{:S(2)}, u32[]{:S(2)}) collective-permute-start(f32[2,14592]{1,0:T(2,128)S(1)} %reshape.294), channel_id=1, source_target_pairs={{0,1},{2,3},{4,5},{6,7},{8,9},{10,11},{12,13},{14,15},{16,17},{18,... | collective-permute-start | bytes 350216 | tf_op jit(solution)/shard_map/ppermute | solution.py:14
  76.3 2.5 %copy-start.2 = (f32[2,256,256]{2,1,0:T(8,128)S(1)}, f32[2,256,256]{2,1,0:T(8,128)}, u32[]{:S(2)}) copy-start(f32[2,256,256]{2,1,0:T(8,128)} %param.13) | copy-start | bytes 1572868
  76.5 2.4 %collective-permute-start.1 = (f32[2,12288]{1,0:T(2,128)S(1)}, f32[2,12288]{1,0:T(2,128)S(1)}, u32[]{:S(2)}, u32[]{:S(2)}) collective-permute-start(f32[2,12288]{1,0:T(2,128)S(1)} %bitcast.80), channel_id=1, source_target_pairs={{0,2},{2,4},{4,6},{1,3},{3,5},{5,7},{8,10},{10,12},{12,14},{9,11},... | collective-permute-start | bytes 294920 | tf_op jit(solution)/shard_map/ppermute | solution.py:14
  78.9 3.3 %copy-start.1 = (f32[2,256,256]{2,1,0:T(8,128)}, f32[2,256,256]{2,1,0:T(8,128)S(1)}, u32[]{:S(2)}) copy-start(f32[2,256,256]{2,1,0:T(8,128)S(1)} %slice_subtract_fusion) | copy-start | bytes 1572868
Sparse Core Ops, SparseCore 0:
  82.4 32.1 reduce-scatter.1
where the time goes:
time: 122 us; the launch traced here: 121 us
  waiting for transfers between devices  41.7 us (34%)
  matrix products  27.9 us (23%)
  local copies, waits for them, and re-layouts  18.2 us (15%)
  between operations  14.2 us (12%)
  starting transfers between devices  12.4 us (10%)
  other arithmetic  6.25 us (5%)
    reduce_scatter x1, waiting for transfers between devices, per_device(): lax.psum_scatter(jnp.einsum('bt,byx->tyx', fit_weight, residual, precisio...  32.3 us
    dot_general x16, matrix products, step(): jnp.einsum('hk,bkw->bhw', row_table, placed, preferred_element_type=jnp.f...  20.4 us
    reshape x16, local copies, waits for them, and re-layouts, step(): patch_four = patch_blk.reshape(block, bands_here, PATCH, PATCH)  8.79 us
    dot_general x16, matrix products, make_patches(): jnp.einsum('sk,bkp->sbp', coef, psf_local.astype(jnp.float32), precision=...  5.34 us
    all_to_all x1, starting transfers between devices, per_device(): lax.all_to_all(packed, ('ty', 'tx'), split_axis=0, concat_axis=0, tiled=T...  5.17 us
    ppermute x2, starting transfers between devices, passed_along(): lax.ppermute(value, axis, [(source, source + steps) for source in range(i...  3.91 us
    all_to_all x1, waiting for transfers between devices, per_device(): lax.all_to_all(amps_send, ('ty', 'tx'), split_axis=0, concat_axis=0, tile...  3.4 us
    all_to_all x1, starting transfers between devices, per_device(): lax.all_to_all(amps_send, ('ty', 'tx'), split_axis=0, concat_axis=0, tile...  3.31 us
  transfers between devices with their start and end apart: 5, of which 5 were waited for; matrix products, arithmetic and copies ran while one was open for 2% of the time, Pallas kernels for 0%

commit v1 on v0

v1 whole, which is shorter than its diff:
```python
import math, functools
import jax, jax.numpy as jnp
from jax import lax
from jax.experimental import pallas as pl
from jax.experimental.pallas import tpu as pltpu
from jax.sharding import PartitionSpec as P
LANES=128; HALF=64; U=4

def pick(flat, first, dest, lane):
    c, off = divmod(first, LANES)
    a = flat[:, c*LANES:(c+1)*LANES]
    if off + 48 > LANES:
        a = jnp.where(lane >= off, a, flat[:, (c+1)*LANES:(c+2)*LANES])
    sh = (dest - off) % LANES
    return pltpu.roll(a, sh, 1) if sh else a

def pack_kernel(psf_ref, out_ref, *, patch):
    kk = psf_ref.shape[1]
    b0 = psf_ref[0].astype(jnp.float32); b1 = psf_ref[1].astype(jnp.float32)
    lane = lax.broadcasted_iota(jnp.int32, (kk, LANES), 1)
    for u in range(patch):
        v = jnp.where(lane < HALF, pick(b0, u*patch, 0, lane), pick(b1, u*patch, HALF, lane))
        out_ref[pl.ds(u, kk, stride=patch), :] = jnp.where(lane % HALF < patch, v, 0.0)

def pack_half_kernel(psi_ref, out_ref, *, patch):
    kk = psi_ref.shape[0]
    b0 = psi_ref[...]
    h = patch//2
    lane = lax.broadcasted_iota(jnp.int32, (kk, LANES), 1)
    for u in range(h):
        v = jnp.where(lane < HALF, pick(b0, u*patch, 0, lane), pick(b0, (u+h)*patch, HALF, lane))
        out_ref[pl.ds(u, kk, stride=h), :] = jnp.where(lane % HALF < patch, v, 0.0)

def render_kernel(feat_ref, ints_ref, amps_ref, g_ref, gt_ref, dirty_ref, res_ref, tay_ref,
                  ints_s, amps_s, list_v, list_s, acc, acct, sems, *, patch, tile, taylor, scales):
    rows = tile + 2*patch
    S = feat_ref.shape[1]
    c1 = pltpu.make_async_copy(ints_ref, ints_s, sems.at[0]); c1.start()
    c2 = pltpu.make_async_copy(amps_ref, amps_s, sems.at[1]); c2.start()
    for j in range(1, acc.shape[0]//rows - 1):
        acc[pl.ds(j*rows+patch, tile), :] = jnp.zeros((tile, LANES), jnp.float32)
        acct[pl.ds(j*rows+patch-patch//2, tile+patch//2), :] = jnp.zeros((tile+patch//2, LANES), jnp.float32)
    rr = feat_ref[0]; cc = feat_ref[1]
    mask = (rr > -patch) & (rr < tile) & (cc > -patch) & (cc < tile)
    mf = jnp.where(mask, 1.0, 0.0)
    i0 = lax.broadcasted_iota(jnp.int32, (LANES, LANES), 0)
    i1 = lax.broadcasted_iota(jnp.int32, (LANES, LANES), 1)
    upper = jnp.where(i0 < i1, 1.0, 0.0).astype(jnp.bfloat16)
    ones = jnp.ones((LANES, LANES), jnp.bfloat16)
    sl = jnp.where(lax.broadcasted_iota(jnp.int32, (S, S), 1) < lax.broadcasted_iota(jnp.int32, (S, S), 0), 1.0, 0.0).astype(jnp.bfloat16)
    mb = mf.astype(jnp.bfloat16)
    f32 = jnp.float32
    before = jnp.dot(sl, mb, preferred_element_type=f32)
    rank = jnp.dot(mb, upper, preferred_element_type=f32) + jnp.dot(before.astype(jnp.bfloat16), ones, preferred_element_type=f32)
    total = jnp.dot(jnp.ones((8, S), jnp.bfloat16), mb, preferred_element_type=f32)
    total = jnp.dot(total.astype(jnp.bfloat16), ones, preferred_element_type=f32)
    rank_i = jnp.where(mask, rank, -1.0).astype(jnp.int32)
    lo = rank_i & (LANES-1)
    hi = jnp.where(mask, rank_i >> 7, -1)
    lane_row = lax.broadcasted_iota(jnp.int32, (S, LANES), 1).astype(f32)
    srow = lax.broadcasted_iota(jnp.int32, (S, LANES), 0)
    flat_i = jnp.zeros((S, LANES), f32); flat_d = jnp.zeros((S, LANES), f32)
    for d in range(S):
        hit = (hi[d:d+1, :] == srow)
        onehot = jnp.where(lo[d:d+1, :] == i0, 1.0, 0.0).astype(jnp.bfloat16)
        lhs = jnp.concatenate([jnp.where(hit, lane_row, 0.0), jnp.where(hit, float(d), 0.0)], 0).astype(jnp.bfloat16)
        got = lax.dot_general(lhs, onehot, (((1,), (1,)), ((), ())), preferred_element_type=f32)
        flat_i += got[:S]; flat_d += got[S:]
    list_v[0:S, :] = flat_d.astype(jnp.int32)*LANES + flat_i.astype(jnp.int32)
    list_v[S:S+8, :] = total.astype(jnp.int32)
    c3 = pltpu.make_async_copy(list_v, list_s, sems.at[2]); c3.start()
    c1.wait(); c2.wait(); c3.wait()
    n = list_s[S, 0]
    lane = lax.broadcasted_iota(jnp.int32, (1, LANES), 1)
    lane_half = lane & (HALF-1)
    h = patch//2

    def gen(i):
        idx = list_s[i >> 7, i & 127]
        idx = jnp.where(i < n, idx, S*LANES)
        row = (idx >> 7)*4; col = idx & 127
        base = ints_s[row, col]; shift = ints_s[row+1, col]; sc = ints_s[row+2, col]
        a = [amps_s[row+t, col] for t in range(taylor)]
        p = None; q = None
        for t in range(taylor):
            k = t*scales + sc
            g = g_ref[pl.ds(pl.multiple_of(k*patch, 8), patch), :]
            gt = gt_ref[pl.ds(pl.multiple_of(k*h, 8), h), :]
            p = a[t]*g if p is None else p + a[t]*g
            q = a[t]*gt if q is None else q + a[t]*gt
        p = p.astype(jnp.bfloat16).astype(f32)
        return (pltpu.roll(p, shift, 1), pltpu.roll(q, shift, 1), base, shift & (HALF-1))

    def put(item):
        p, q, base, w = item
        first = lane_half >= w
        for ref, val, hh in ((acc, p, patch), (acct, q, h)):
            b1 = pl.ds(base, hh); b2 = pl.ds(base + rows, hh)
            ref[b1, :] = ref[b1, :] + jnp.where(first, val, 0.0)
            ref[b2, :] = ref[b2, :] + jnp.where(first, 0.0, val)

    def step(i, carry):
        nxt = tuple(gen((i+1)*U + k) for k in range(U))
        for item in carry: put(item)
        return nxt
    last = lax.fori_loop(0, (n + U - 1)//U, step, tuple(gen(k) for k in range(U)))

    left = lax.broadcasted_iota(jnp.int32, (tile, LANES), 1) < HALF
    for c in range(tile//LANES):
        j = 2*c + 1
        def get(ref, jj, r0): return ref[pl.ds(jj*rows + r0, tile), :]
        x = get(acc, j, patch); y = get(acc, j+1, patch)
        res_ref[0, :, c*LANES:(c+1)*LANES] = dirty_ref[0, :, c*LANES:(c+1)*LANES] - jnp.where(left, x, y)
        res_ref[1, :, c*LANES:(c+1)*LANES] = dirty_ref[1, :, c*LANES:(c+1)*LANES] - pltpu.roll(jnp.where(left, y, x), HALF, 1)
        up = jnp.where(left, get(acct, j, patch), get(acct, j+1, patch))
        low = pltpu.roll(jnp.where(left, get(acct, j+1, patch-h), get(acct, j, patch-h)), HALF, 1)
        tay_ref[0, :, c*LANES:(c+1)*LANES] = up + low

def pack(psf, patch):
    return pl.pallas_call(functools.partial(pack_kernel, patch=patch),
        out_shape=jax.ShapeDtypeStruct((psf.shape[1]*patch, LANES), jnp.float32))(psf)
def pack_half(psi, patch):
    return pl.pallas_call(functools.partial(pack_half_kernel, patch=patch),
        out_shape=jax.ShapeDtypeStruct((psi.shape[0]*(patch//2), LANES), jnp.float32))(psi)

def render(feats, g, gt, dirty, r0, c0, *, patch, taylor, scales):
    tile = dirty.shape[1]; rows = tile + 2*patch; S = feats.shape[0]
    tiles = tile//HALF + 2
    rr = feats[:, 0] - r0; cc = feats[:, 1] - c0
    fz = jnp.stack([rr, cc])
    ri = jnp.clip(rr.astype(jnp.int32), -patch, tile) + patch
    ci = jnp.clip(cc.astype(jnp.int32), -HALF, tile - 1)
    base = ((ci + HALF)//HALF)*rows + ri
    base = jnp.minimum(base, (tiles-1)*rows - patch)
    ints = jnp.stack([base, ci & (LANES-1), feats[:, 2].astype(jnp.int32), jnp.zeros_like(base)], 1)
    amps = feats[:, 3:3+taylor]
    ints = jnp.concatenate([ints, jnp.zeros((1,)+ints.shape[1:], jnp.int32)], 0).reshape(-1, LANES)
    amps = jnp.concatenate([amps, jnp.zeros((1,)+amps.shape[1:], jnp.float32)], 0).reshape(-1, LANES)
    V = pl.BlockSpec(memory_space=pltpu.VMEM)
    f32 = jnp.float32
    return pl.pallas_call(
        functools.partial(render_kernel, patch=patch, tile=tile, taylor=taylor, scales=scales),
        out_shape=(jax.ShapeDtypeStruct(dirty.shape, f32), jax.ShapeDtypeStruct((1,)+dirty.shape[1:], f32)),
        in_specs=[V]*6, out_specs=(V, V),
        scratch_shapes=[pltpu.SMEM(ints.shape, jnp.int32), pltpu.SMEM(amps.shape, f32),
            pltpu.VMEM((S+8, LANES), jnp.int32), pltpu.SMEM((S+8, LANES), jnp.int32),
            pltpu.VMEM((tiles*rows, LANES), f32), pltpu.VMEM((tiles*rows, LANES), f32),
            pltpu.SemaphoreType.DMA((3,))],
        compiler_params=pltpu.CompilerParams(vmem_limit_bytes=32*1024*1024),
    )(fz, ints, amps, g, gt, dirty)


def doubled(value, axes, size):
    held = value[None]
    bit = 1
    while bit < size:
        other = lax.ppermute(held, axes, [(i, i ^ bit) for i in range(size)])
        held = jnp.concatenate([held, other], 0)
        bit *= 2
    return held


def per_device(dirty, psf, comp_tile, comp_offset, comp_scale, comp_amp, fit_weight):
    bands_here, tile = dirty.shape[0], dirty.shape[1]
    patch = math.isqrt(psf.shape[2])
    taylor = comp_amp.shape[1]
    scales = psf.shape[1] // taylor
    n_ty, n_tx, n_band = lax.axis_size("ty"), lax.axis_size("tx"), lax.axis_size("band")
    ty, tx, me = lax.axis_index("ty"), lax.axis_index("tx"), lax.axis_index("band")
    f32 = jnp.float32
    where_tile = comp_tile[:, 0]
    row = (where_tile // n_tx) * tile + comp_offset[:, 0]
    col = (where_tile % n_tx) * tile + comp_offset[:, 1]
    ints = jnp.stack([row, col, comp_scale], 0).astype(f32)
    feats = jnp.concatenate([ints, comp_amp.T, jnp.zeros((8 - 3 - taylor, row.shape[0]), f32)], 0)
    lift = 2.0 ** math.floor(math.log2(60000.0 / (bands_here * 30.0)))

    def weighted(values, step):
        w = lax.dynamic_slice_in_dim(fit_weight, me ^ step, 1, 1)[:, 0]
        total = w[0] * values[0].astype(f32)
        for b in range(1, bands_here):
            total = total + w[b] * values[b].astype(f32)
        return total

    def summed(values):
        total = weighted(values, 0)
        for step in range(1, n_band):
            part = (weighted(values, step) * lift).astype(jnp.float16)
            got = lax.ppermute(part, "band", [(i, i ^ step) for i in range(n_band)])
            total = total + got.astype(f32) * (1.0 / lift)
        return total

    everyone = doubled(feats, ("ty", "tx"), n_ty * n_tx)
    psi = summed(psf)
    dirty_fit = summed(dirty)
    residual, model_fit = render(
        everyone, pack(psf, patch), pack_half(psi, patch), dirty,
        (ty * tile).astype(f32), (tx * tile).astype(f32),
        patch=patch, taylor=taylor, scales=scales)
    return residual, dirty_fit[None] - model_fit


def solution(mesh):
    return jax.shard_map(
        per_device,
        mesh=mesh,
        in_specs=(
            P("band", "ty", "tx"),
            P("band", None, None),
            P(("ty", "tx"), None),
            P(("ty", "tx"), None),
            P(("ty", "tx")),
            P(("ty", "tx"), None),
            P("band", None),
        ),
        out_specs=(P("band", "ty", "tx"), P("band", "ty", "tx")),
        check_vma=False,
    )
```

time: 122 us -> 46.1 us (0.38)
  waiting for transfers between devices: 41.7 us -> 0.02 us
  matrix products: 27.9 us -> 0 us
  between operations: 14.2 us -> 0.87 us
  Pallas kernels: 0 us -> 13.1 us
  local copies, waits for them, and re-layouts: 18.2 us -> 5.87 us
  other arithmetic: 6.25 us -> 12.3 us
    reduce_scatter x1 -> x0, waiting for transfers between devices: 32.3 us -> none  [per_device(): lax.psum_scatter(jnp.einsum('bt,byx->tyx', fit_weight, residual, precisio...]
    dot_general x33 -> x0, matrix products: 27.9 us -> none  [the longest x16 20.4 us: step(): jnp.einsum('hk,bkw->bhw', row_table, placed, preferred_element_type=jnp.f...]
    pallas_call x0 -> x3, Pallas kernels: none -> 13.1 us  [the longest x1 9.32 us: render(): pl.pallas_call(functools.partial(render_kernel, patch=patch, tile=tile, t...]
    ppermute x2 -> x9, starting transfers between devices: 3.91 us -> 13.6 us  [the longest x6 8.97 us: summed(): got = lax.ppermute(part, 'band', [(i, i ^ step) for i in range(n_band)])]
    reshape x17 -> x2, local copies, waits for them, and re-layouts: 9.03 us -> 0.02 us  [the longest x1 0.01 us: render(): jnp.concatenate([amps, jnp.zeros((1,) + amps.shape[1:], jnp.float32)], 0)]
    all_to_all x2 -> x0, starting transfers between devices: 8.48 us -> none  [the longest x1 5.17 us: per_device(): lax.all_to_all(packed, ('ty', 'tx'), split_axis=0, concat_axis=0, tiled=T...]
    all_to_all x2 -> x0, waiting for transfers between devices: 6.43 us -> none  [the longest x1 3.4 us: per_device(): lax.all_to_all(amps_send, ('ty', 'tx'), split_axis=0, concat_axis=0, tile...]
    convert_element_type x16 -> x3, other arithmetic: 0.12 us -> 3.98 us  [the longest x1 3.96 us: summed(): part = (weighted(values, step) * lift).astype(jnp.float16)]
  transfers between devices with their start and end apart: 5 -> 9, of which waited for: 5 -> 0; matrix products, arithmetic and copies ran while one was open for 2% -> 27% of each run, Pallas kernels for 0% -> 29%
where the time goes in v1:
time: 46.1 us; the launch traced here: 45.7 us
  starting transfers between devices  13.6 us (30%)
  Pallas kernels  13.1 us (28%)
  other arithmetic  12.3 us (27%)
  local copies, waits for them, and re-layouts  5.87 us (13%)
  between operations  0.87 us (2%)
    pallas_call x1, Pallas kernels, render(): pl.pallas_call(functools.partial(render_kernel, patch=patch, tile=tile, t...  9.32 us
    ppermute x6, starting transfers between devices, summed(): got = lax.ppermute(part, 'band', [(i, i ^ step) for i in range(n_band)])  8.97 us
    ppermute x3, starting transfers between devices, doubled(): other = lax.ppermute(held, axes, [(i, i ^ bit) for i in range(size)])  4.6 us
    unnamed x23, local copies, waits for them, and re-layouts  4.51 us
    convert_element_type x1, other arithmetic, summed(): part = (weighted(values, step) * lift).astype(jnp.float16)  3.96 us
    mul x1, other arithmetic, summed(): part = (weighted(values, step) * lift).astype(jnp.float16)  3.95 us
    sub x1, other arithmetic, per_device(): return (residual, dirty_fit[None] - model_fit)  2.1 us
    add x1, other arithmetic, summed(): total = total + got.astype(f32) * (1.0 / lift)  2.09 us
  transfers between devices with their start and end apart: 9, of which 0 were waited for; matrix products, arithmetic and copies ran while one was open for 27% of the time, Pallas kernels for 29%

profile of v1, /device:TPU:0, one launch (start us, length us, event | category | flops | bytes accessed | tf_op | source)
XLA Modules:
  0.0 45.7 jit_solution(16294189091590303880)
XLA Ops:
  0.6 0.1 pad.19.clone
  0.7 0.6 %copy-done.7 = s32[128,2]{0,1:T(2,128)S(1)} copy-done((s32[128,2]{0,1:T(2,128)S(1)}, s32[128,2]{0,1:T(2,128)}, u32[]{:S(2)}) %copy-start.7) | copy-done | bytes 1048
  1.3 0.0 copy-start.9
  1.3 0.6 %copy-done.9 = s32[128]{0:T(128)S(1)} copy-done((s32[128]{0:T(128)S(1)}, s32[128]{0:T(128)}, u32[]{:S(2)}) %copy-start.9) | copy-done | bytes 536
  2.0 0.7 %copy-done.6 = f32[128,4]{0,1:T(4,128)S(1)} copy-done((f32[128,4]{0,1:T(4,128)S(1)}, f32[128,4]{0,1:T(4,128)}, u32[]{:S(2)}) %copy-start.6) | copy-done | bytes 2072
  2.7 0.1 maximum_maximum_fusion
  2.7 2.9 %collective-permute-start = (f32[1,8,128]{2,0,1:T(1,128)S(1)}, f32[1,8,128]{2,0,1:T(1,128)S(1)}, u32[]{:S(2)}, u32[]{:S(2)}) collective-permute-start(f32[1,8,128]{2,0,1:T(1,128)S(1)} %bitcast.65), channel_id=1, source_target_pairs={{0,1},{1,0},{2,3},{3,2},{4,5},{5,4},{6,7},{7,6},{8,9},{9,8},{10,11... | collective-permute-start | bytes 12296 | tf_op jit(solution)/shard_map/ppermute | solution.py:157
  5.7 0.7 %copy-done.5 = f32[2,4]{1,0:T(2,128)S(1)} copy-done((f32[2,4]{1,0:T(2,128)S(1)}, f32[2,4]{1,0:T(2,128)}, u32[]{:S(2)}) %copy-start.5) | copy-done | bytes 56
  6.4 0.1 constant_dynamic-slice_fusion.3
  6.4 0.6 %fusion.30 = (f32[1,1]{1,0:T(1,128)}, f32[1,1]{1,0:T(1,128)}, f32[1,1]{1,0:T(1,128)}, f32[1,1]{1,0:T(1,128)}) fusion(f32[2,1]{1,0:T(2,128)S(1)} %get-tuple-element.19, f32[2,1]{1,0:T(2,128)S(1)} %get-tuple-element.20), kind=kLoop, calls=%fused_computation.72 | loop fusion | bytes 32 | tf_op jit(solution)/shard_map/slice | solution.py:180
  7.0 0.6 %fusion.32 = (f32[1,1]{1,0:T(1,128)}, f32[1,1]{1,0:T(1,128)}, f32[1,1]{1,0:T(1,128)}, f32[1,1]{1,0:T(1,128)}) fusion(f32[2,1]{1,0:T(2,128)S(1)} %get-tuple-element.22, f32[2,1]{1,0:T(2,128)S(1)} %get-tuple-element.21), kind=kLoop, calls=%fused_computation.74 | loop fusion | bytes 32 | tf_op jit(solution)/shard_map/slice | solution.py:180
  7.6 0.9 %copy.11.psf_ref = bf16[2,20,2304]{2,1,0:T(8,128)(2,1)S(1)} copy(bf16[2,20,2304]{2,0,1:T(2,128)(2,1)} %param.8) | data formatting | bytes 368640 | tf_op args[1]
  8.6 0.0 copy-start.3
  8.6 0.0 collective-permute-done
  8.6 0.1 collective-permute-start.1
  8.7 4.0 %fusion.21 = (f16[20,2304]{1,0:T(8,128)(2,1)S(1)}, f16[20,2304]{1,0:T(8,128)(2,1)S(1)}, f16[20,2304]{1,0:T(8,128)(2,1)S(1)}) fusion(f32[]{:T(128)} %bitcast.12, f32[]{:T(128)} %bitcast.11, bf16[2,20,2304]{2,1,0:T(8,128)(2,1)S(1)} %copy.11.psf_ref, f32[]{:T(128)} %bitcast.15, f32[]{:T(128)} %bitcast.14, f32[]{:T(128)} %bitcast.18, f32[]{:T(128)} %bitcast.17), kind=kLoop, calls=%fused_computation.34 | loop fusion | flops 783360 | bytes 460824 | tf_op jit(solution)/shard_map/mul | solution.py:188
  12.7 1.6 %collective-permute-start.3 = (f16[20,2304]{1,0:T(8,128)(2,1)S(1)}, f16[20,2304]{1,0:T(8,128)(2,1)S(1)}, u32[]{:S(2)}, u32[]{:S(2)}) collective-permute-start(f16[20,2304]{1,0:T(8,128)(2,1)S(1)} %get-tuple-element.12), channel_id=1, source_target_pairs={{0,8},{8,0},{16,24},{24,16},{1,9},{9,1},{17,25},{25,17},{2,10},{10... | collective-permute-start | bytes 276488 | tf_op jit(solution)/shard_map/ppermute | solution.py:189
  14.3 2.6 %collective-permute-start.4 = (f16[20,2304]{1,0:T(8,128)(2,1)S(1)}, f16[20,2304]{1,0:T(8,128)(2,1)S(1)}, u32[]{:S(2)}, u32[]{:S(2)}) collective-permute-start(f16[20,2304]{1,0:T(8,128)(2,1)S(1)} %get-tuple-element.13), channel_id=1, source_target_pairs={{0,16},{8,24},{16,0},{24,8},{1,17},{9,25},{17,1},{25,9},{2,18},{10... | collective-permute-start | bytes 276488 | tf_op jit(solution)/shard_map/ppermute | solution.py:189
  16.9 0.2 collective-permute-start.5
  17.1 0.0 collective-permute-done.1
  17.1 1.6 %collective-permute-start.2 = (f32[4,8,128]{2,0,1:T(4,128)S(1)}, f32[4,8,128]{2,0,1:T(4,128)S(1)}, u32[]{:S(2)}, u32[]{:S(2)}) collective-permute-start(f32[4,8,128]{2,0,1:T(4,128)S(1)} %pad_maximum_fusion.3), channel_id=1, source_target_pairs={{0,4},{1,5},{2,6},{3,7},{4,0},{5,1},{6,2},{7,3},{8,12},{9,13},{10,... | collective-permute-start | bytes 49160 | tf_op jit(solution)/shard_map/ppermute | solution.py:157
  18.7 4.0 %fusion.16 = (f16[256,256]{1,0:T(8,128)(2,1)S(1)}, f16[256,256]{1,0:T(8,128)(2,1)S(1)}, f16[256,256]{1,0:T(8,128)(2,1)S(1)}) fusion(f32[2,256,256]{2,1,0:T(8,128)S(1)} %copy-done, f32[]{:T(128)} %bitcast.12, f32[]{:T(128)} %bitcast.11, f32[]{:T(128)} %bitcast.15, f32[]{:T(128)} %bitcast.14, f32[]{:T(128)} %bitcast.18, f32[]{:T(128)} %bitcast.17), kind=kLoop, calls=%fused_computation.29 | loop fusion | flops 983040 | bytes 917528 | tf_op jit(solution)/shard_map/convert_element_type | solution.py:188
  22.7 0.7 %collective-permute-start.6 = (f16[256,256]{1,0:T(8,128)(2,1)S(1)}, f16[256,256]{1,0:T(8,128)(2,1)S(1)}, u32[]{:S(2)}, u32[]{:S(2)}) collective-permute-start(f16[256,256]{1,0:T(8,128)(2,1)S(1)} %get-tuple-element.9), channel_id=1, source_target_pairs={{0,8},{8,0},{16,24},{24,16},{1,9},{9,1},{17,25},{25,17},{2,10},{10... | collective-permute-start | bytes 393224 | tf_op jit(solution)/shard_map/ppermute | solution.py:189
  23.4 1.9 %shard_map.86.g_ref = f32[960,128]{1,0:T(8,128)} custom-call(bf16[2,20,2304]{2,1,0:T(8,128)(2,1)} %copy-done.3), custom_call_target="tpu_custom_call" | custom-call | tf_op jit(solution)/shard_map/pallas_call | solution.py:120
  25.4 3.5 %collective-permute-start.7 = (f16[256,256]{1,0:T(8,128)(2,1)S(1)}, f16[256,256]{1,0:T(8,128)(2,1)S(1)}, u32[]{:S(2)}, u32[]{:S(2)}) collective-permute-start(f16[256,256]{1,0:T(8,128)(2,1)S(1)} %get-tuple-element.10), channel_id=1, source_target_pairs={{0,16},{8,24},{16,0},{24,8},{1,17},{9,25},{17,1},{25,9},{2,18},{10... | collective-permute-start | bytes 393224 | tf_op jit(solution)/shard_map/ppermute | solution.py:189
  29.1 0.3 collective-permute-start.8
  29.4 0.0 copy-start.1
  29.4 2.1 %fusion.6.psi_ref = f32[20,2304]{1,0:T(8,128)} fusion(f16[20,2304]{1,0:T(8,128)(2,1)S(1)} %collective-permute-done.5, f16[20,2304]{1,0:T(8,128)(2,1)S(1)} %collective-permute-done.4, f16[20,2304]{1,0:T(8,128)(2,1)S(1)} %collective-permute-done.3, f32[]{:T(128)} %bitcast.9, f32[]{:T(128)} %bitcast.8, bf16[2,20,2304]{2,1,0:T(8,128)(2,1)S(1)} %copy-done.4), kind=kLoop, calls=%fused_computation.19 | loop fusion | flops 645120 | bytes 645128 | tf_op jit(solution)/shard_map/add | solution.py:190
  31.5 1.8 %shard_map.87.gt_ref = f32[480,128]{1,0:T(8,128)} custom-call(f32[20,2304]{1,0:T(8,128)} %fusion.6.psi_ref), custom_call_target="tpu_custom_call" | custom-call | tf_op jit(solution)/shard_map/pallas_call | solution.py:123
  33.3 0.9 %copy-done.2 = f32[480,128]{1,0:T(8,128)S(1)} copy-done((f32[480,128]{1,0:T(8,128)S(1)}, f32[480,128]{1,0:T(8,128)}, u32[]{:S(2)}) %copy-start.2) | copy-done | bytes 245784
  34.3 9.3 %shard_map.88 = (f32[2,256,256]{2,1,0:T(8,128)}, f32[1,256,256]{2,1,0:T(8,128)S(1)}) custom-call(f32[2,8,128]{2,1,0:T(8,128)S(1)} %pad_maximum_fusion.5.feat_ref, s32[36,128]{1,0:T(8,128)S(1)} %reshape.238.ints_ref, f32[36,128]{1,0:T(8,128)S(1)} %reshape.239.amps_ref, f32[960,128]{1,0:T(8,128)S(1)} %copy-done.1, f32[480,128]{1,0:T(8,128)S(1)} %copy-done.2, ...), custom_call_target="tpu_custom_call" | custom-call | tf_op jit(solution)/shard_map/pallas_call | solution.py:141
  43.6 2.1 %bitcast_subtract_fusion = f32[1,256,256]{2,1,0:T(8,128)} fusion(f32[1,256,256]{2,1,0:T(8,128)S(1)} %get-tuple-element.5, f16[256,256]{1,0:T(8,128)(2,1)S(1)} %collective-permute-done.8, f16[256,256]{1,0:T(8,128)(2,1)S(1)} %collective-permute-done.7, f16[256,256]{1,0:T(8,128)(2,1)S(1)} %collective-permute-done.6, f32[2,256,256]{2,1,0:T(8,128)S(1)} %copy-done, ...), kind=kLoop, calls=%fused_computation.8 | loop fusion | flops 851968 | bytes 1441800 | tf_op jit(solution)/shard_map/sub | solution.py:200
  (36 shorter events, 0.2 us)
Async XLA Ops:
  0.6 0.7 %copy-start.7 = (s32[128,2]{0,1:T(2,128)S(1)}, s32[128,2]{0,1:T(2,128)}, u32[]{:S(2)}) copy-start(s32[128,2]{0,1:T(2,128)} %param.10) | copy-start | bytes 3076
  0.6 0.7 %copy-start.8 = (s32[128,1]{0,1:T(1,128)S(1)}, s32[128,1]{0,1:T(1,128)}, u32[]{:S(2)}) copy-start(s32[128,1]{0,1:T(1,128)} %param.9) | copy-start | bytes 1540
  1.3 0.7 %copy-start.9 = (s32[128]{0:T(128)S(1)}, s32[128]{0:T(128)}, u32[]{:S(2)}) copy-start(s32[128]{0:T(128)} %param.11) | copy-start | bytes 1540
  2.0 0.7 %copy-start.6 = (f32[128,4]{0,1:T(4,128)S(1)}, f32[128,4]{0,1:T(4,128)}, u32[]{:S(2)}) copy-start(f32[128,4]{0,1:T(4,128)} %param.12) | copy-start | bytes 6148
  2.7 5.8 %collective-permute-start = (f32[1,8,128]{2,0,1:T(1,128)S(1)}, f32[1,8,128]{2,0,1:T(1,128)S(1)}, u32[]{:S(2)}, u32[]{:S(2)}) collective-permute-start(f32[1,8,128]{2,0,1:T(1,128)S(1)} %bitcast.65), channel_id=1, source_target_pairs={{0,1},{1,0},{2,3},{3,2},{4,5},{5,4},{6,7},{7,6},{8,9},{9,8},{10,11... | collective-permute-start | bytes 12296 | tf_op jit(solution)/shard_map/ppermute | solution.py:157
  5.7 0.7 %copy-start.5 = (f32[2,4]{1,0:T(2,128)S(1)}, f32[2,4]{1,0:T(2,128)}, u32[]{:S(2)}) copy-start(f32[2,4]{1,0:T(2,128)} %param.13) | copy-start | bytes 100
  7.0 11.7 %copy-start = (f32[2,256,256]{2,1,0:T(8,128)S(1)}, f32[2,256,256]{2,1,0:T(8,128)}, u32[]{:S(2)}) copy-start(f32[2,256,256]{2,1,0:T(8,128)} %dirty_ref.1) | copy-start | bytes 1572868
  8.6 4.1 %copy-start.3 = (bf16[2,20,2304]{2,1,0:T(8,128)(2,1)}, bf16[2,20,2304]{2,1,0:T(8,128)(2,1)S(1)}, u32[]{:S(2)}) copy-start(bf16[2,20,2304]{2,1,0:T(8,128)(2,1)S(1)} %copy.11.psf_ref) | copy-start | bytes 552964
  8.6 8.5 %collective-permute-start.1 = (f32[2,8,128]{2,0,1:T(2,128)S(1)}, f32[2,8,128]{2,0,1:T(2,128)S(1)}, u32[]{:S(2)}, u32[]{:S(2)}) collective-permute-start(f32[2,8,128]{2,0,1:T(2,128)S(1)} %pad_maximum_fusion.4), channel_id=1, source_target_pairs={{0,2},{1,3},{2,0},{3,1},{4,6},{5,7},{6,4},{7,5},{8,10},{9,11},{10,... | collective-permute-start | bytes 24584 | tf_op jit(solution)/shard_map/ppermute | solution.py:157
  12.7 16.4 %collective-permute-start.3 = (f16[20,2304]{1,0:T(8,128)(2,1)S(1)}, f16[20,2304]{1,0:T(8,128)(2,1)S(1)}, u32[]{:S(2)}, u32[]{:S(2)}) collective-permute-start(f16[20,2304]{1,0:T(8,128)(2,1)S(1)} %get-tuple-element.12), channel_id=1, source_target_pairs={{0,8},{8,0},{16,24},{24,16},{1,9},{9,1},{17,25},{25,17},{2,10},{10... | collective-permute-start | bytes 276488 | tf_op jit(solution)/shard_map/ppermute | solution.py:189
  14.3 15.1 %collective-permute-start.4 = (f16[20,2304]{1,0:T(8,128)(2,1)S(1)}, f16[20,2304]{1,0:T(8,128)(2,1)S(1)}, u32[]{:S(2)}, u32[]{:S(2)}) collective-permute-start(f16[20,2304]{1,0:T(8,128)(2,1)S(1)} %get-tuple-element.13), channel_id=1, source_target_pairs={{0,16},{8,24},{16,0},{24,8},{1,17},{9,25},{17,1},{25,9},{2,18},{10... | collective-permute-start | bytes 276488 | tf_op jit(solution)/shard_map/ppermute | solution.py:189
  16.9 12.5 %collective-permute-start.5 = (f16[20,2304]{1,0:T(8,128)(2,1)S(1)}, f16[20,2304]{1,0:T(8,128)(2,1)S(1)}, u32[]{:S(2)}, u32[]{:S(2)}) collective-permute-start(f16[20,2304]{1,0:T(8,128)(2,1)S(1)} %get-tuple-element.14), channel_id=1, source_target_pairs={{0,24},{8,16},{16,8},{24,0},{1,25},{9,17},{17,9},{25,1},{2,26},{10... | collective-permute-start | bytes 276488 | tf_op jit(solution)/shard_map/ppermute | solution.py:189
  17.1 8.2 %collective-permute-start.2 = (f32[4,8,128]{2,0,1:T(4,128)S(1)}, f32[4,8,128]{2,0,1:T(4,128)S(1)}, u32[]{:S(2)}, u32[]{:S(2)}) collective-permute-start(f32[4,8,128]{2,0,1:T(4,128)S(1)} %pad_maximum_fusion.3), channel_id=1, source_target_pairs={{0,4},{1,5},{2,6},{3,7},{4,0},{5,1},{6,2},{7,3},{8,12},{9,13},{10,... | collective-permute-start | bytes 49160 | tf_op jit(solution)/shard_map/ppermute | solution.py:157
  22.7 20.9 %collective-permute-start.6 = (f16[256,256]{1,0:T(8,128)(2,1)S(1)}, f16[256,256]{1,0:T(8,128)(2,1)S(1)}, u32[]{:S(2)}, u32[]{:S(2)}) collective-permute-start(f16[256,256]{1,0:T(8,128)(2,1)S(1)} %get-tuple-element.9), channel_id=1, source_target_pairs={{0,8},{8,0},{16,24},{24,16},{1,9},{9,1},{17,25},{25,17},{2,10},{10... | collective-permute-start | bytes 393224 | tf_op jit(solution)/shard_map/ppermute | solution.py:189
  25.4 4.0 %copy-start.4 = (bf16[2,20,2304]{2,1,0:T(8,128)(2,1)S(1)}, bf16[2,20,2304]{2,1,0:T(8,128)(2,1)}, u32[]{:S(2)}) copy-start(bf16[2,20,2304]{2,1,0:T(8,128)(2,1)} %copy-done.3) | copy-start | bytes 552964
  25.4 18.2 %collective-permute-start.7 = (f16[256,256]{1,0:T(8,128)(2,1)S(1)}, f16[256,256]{1,0:T(8,128)(2,1)S(1)}, u32[]{:S(2)}, u32[]{:S(2)}) collective-permute-start(f16[256,256]{1,0:T(8,128)(2,1)S(1)} %get-tuple-element.10), channel_id=1, source_target_pairs={{0,16},{8,24},{16,0},{24,8},{1,17},{9,25},{17,1},{25,9},{2,18},{10... | collective-permute-start | bytes 393224 | tf_op jit(solution)/shard_map/ppermute | solution.py:189
  29.1 14.5 %collective-permute-start.8 = (f16[256,256]{1,0:T(8,128)(2,1)S(1)}, f16[256,256]{1,0:T(8,128)(2,1)S(1)}, u32[]{:S(2)}, u32[]{:S(2)}) collective-permute-start(f16[256,256]{1,0:T(8,128)(2,1)S(1)} %get-tuple-element.11), channel_id=1, source_target_pairs={{0,24},{8,16},{16,8},{24,0},{1,25},{9,17},{17,9},{25,1},{2,26},{10... | collective-permute-start | bytes 393224 | tf_op jit(solution)/shard_map/ppermute | solution.py:189
  29.4 3.9 %copy-start.1 = (f32[960,128]{1,0:T(8,128)S(1)}, f32[960,128]{1,0:T(8,128)}, u32[]{:S(2)}) copy-start(f32[960,128]{1,0:T(8,128)} %shard_map.86.g_ref) | copy-start | bytes 1474564
  33.3 0.9 %copy-start.2 = (f32[480,128]{1,0:T(8,128)S(1)}, f32[480,128]{1,0:T(8,128)}, u32[]{:S(2)}) copy-start(f32[480,128]{1,0:T(8,128)} %shard_map.87.gt_ref) | copy-start | bytes 737284

commit v2 on v0

v2 whole, which is shorter than its diff:
```python
import functools
import math
import jax
import jax.numpy as jnp
from jax import lax
from jax.experimental import pallas as pl
from jax.experimental.pallas import tpu as pltpu
from jax.sharding import PartitionSpec as P

LANES = 128
HALF = 64
U = 16
F32, BF16, I32 = jnp.float32, jnp.bfloat16, jnp.int32


def vmem():
    return pl.BlockSpec(memory_space=pltpu.VMEM)


def prep_kernel(w_hbm, tile_hbm, offset_hbm, scale_hbm, amp_hbm, dirty_hbm, psf_hbm,
                feat_ref, dpart_ref, ppart_ref, plane_ref,
                w_ref, tile_ref, offset_ref, scale_ref, amp_ref, dirty_ref, psf_ref, pairs, psi, sems, *,
                me, half, n_tx, n_band):
    copies = [pltpu.make_async_copy(src, dst, sems.at[i]) for i, (src, dst) in enumerate((
        (psf_hbm, psf_ref), (w_hbm, w_ref), (tile_hbm, tile_ref), (offset_hbm, offset_ref),
        (scale_hbm, scale_ref), (amp_hbm, amp_ref), (dirty_hbm, dirty_ref)))]
    for copy in copies:
        copy.start()
    bands, side = dirty_ref.shape[0], dirty_ref.shape[1]
    kk, flat = psf_ref.shape[0], psf_ref.shape[2]
    taylor = amp_ref.shape[0]
    me, half = me(), half()
    part, deep = kk // 2, -(-kk // 8) * 8
    copies[0].wait()
    copies[1].wait()
    for c in range(flat // LANES):
        cols = slice(c * LANES, (c + 1) * LANES)
        top = c * bands * kk
        for k in range(kk):
            pairs[top + bands * k:top + bands * (k + 1), :] = psf_ref[k, :, cols].astype(F32)
    planes = {}
    for c in range(flat // LANES):
        for b in range(bands):
            planes[b, c] = pairs[pl.ds(c * bands * kk + b, kk, stride=bands), :]
            plane_ref[b, :, c * LANES:(c + 1) * LANES] = planes[b, c]
    for step in range(n_band):
        to = me ^ step
        for c in range(flat // LANES):
            total = w_ref[0, to] * planes[0, c]
            for b in range(1, bands):
                total = total + w_ref[b, to] * planes[b, c]
            psi[(step * (flat // LANES) + c) * deep:(step * (flat // LANES) + c) * deep + kk, :] = total
    for step in range(n_band):
        for c in range(flat // LANES):
            top = (step * (flat // LANES) + c) * deep
            ppart_ref[step, c * part:(c + 1) * part, :] = psi[pl.ds(top + half * part, part), :]
    for copy in copies[2:]:
        copy.wait()
    tile = tile_ref[0:1, :]
    feat_ref[0] = ((tile // n_tx) * side + offset_ref[0:1, :]).astype(F32)
    feat_ref[1] = ((tile % n_tx) * side + offset_ref[1:2, :]).astype(F32)
    feat_ref[2] = scale_ref[0:1, :].astype(F32)
    for t in range(taylor):
        feat_ref[3 + t] = amp_ref[t:t + 1, :]
    for step in range(n_band):
        to = me ^ step
        total = w_ref[0, to] * dirty_ref[0]
        for b in range(1, bands):
            total = total + w_ref[b, to] * dirty_ref[b]
        dpart_ref[step] = total


def prep(dirty, psf, comp_tile, comp_offset, comp_scale, comp_amp, fit_weight, me, half, n_tx, n_band):
    bands, kk, flat = psf.shape
    listed, taylor = comp_amp.shape
    feats, deep = 3 + taylor, -(-kk // 8) * 8
    rows = (kk // 2) * (flat // LANES)
    args = (fit_weight, comp_tile.T, comp_offset.T, comp_scale[None], comp_amp.T, dirty, psf.transpose(1, 0, 2))
    return pl.pallas_call(
        functools.partial(prep_kernel, me=me, half=half, n_tx=n_tx, n_band=n_band),
        out_shape=(
            jax.ShapeDtypeStruct((feats, 1, listed), F32),
            jax.ShapeDtypeStruct((n_band,) + dirty.shape[1:], F32),
            jax.ShapeDtypeStruct((n_band, rows, LANES), F32),
            jax.ShapeDtypeStruct(psf.shape, F32),
        ),
        in_specs=[pl.BlockSpec(memory_space=pltpu.HBM)] * len(args),
        out_specs=(vmem(),) * 4,
        scratch_shapes=[pltpu.SMEM(args[0].shape, F32)] + [pltpu.VMEM(x.shape, x.dtype) for x in args[1:]] + [
            pltpu.VMEM((bands * kk * (flat // LANES), LANES), F32),
            pltpu.VMEM((n_band * deep * (flat // LANES), LANES), F32),
            pltpu.SemaphoreType.DMA((len(args),))],
        compiler_params=pltpu.CompilerParams(vmem_limit_bytes=12 * 1024 * 1024),
    )(*[pltpu.with_memory_space_constraint(x, pltpu.HBM) for x in args])


def pick(chunk, first, dest, lane, patch):
    c, off = divmod(first, LANES)
    a = chunk(c)
    if off + patch > LANES:
        a = jnp.where(lane >= off, a, chunk(c + 1))
    turn = (dest - off) % LANES
    return pltpu.roll(a, turn, 1) if turn else a


def pack_kernel(psf_ref, out_ref, *, patch):
    kk = psf_ref.shape[1]
    planes = [psf_ref[b] for b in range(2)]
    lane = lax.broadcasted_iota(I32, (kk, LANES), 1)
    for u in range(patch):
        two = [pick(lambda c, x=x: x[:, c * LANES:(c + 1) * LANES], u * patch, b * HALF, lane, patch)
               for b, x in enumerate(planes)]
        v = jnp.where(lane < HALF, two[0], two[1])
        out_ref[pl.ds(u, kk, stride=patch), :] = jnp.where(lane % HALF < patch, v, 0.0)


def pack(psf, patch):
    return pl.pallas_call(
        functools.partial(pack_kernel, patch=patch),
        out_shape=jax.ShapeDtypeStruct((psf.shape[1] * patch, LANES), F32),
        in_specs=[vmem()], out_specs=vmem(),
        compiler_params=pltpu.CompilerParams(vmem_limit_bytes=4 * 1024 * 1024),
    )(psf)


def pack_fit_kernel(mine_ref, other_ref, out_ref, *, patch, half):
    h = patch // 2
    n = mine_ref.shape[0] // (patch * patch // LANES)
    half = half()
    lane = lax.broadcasted_iota(I32, (n, LANES), 1)
    for ref, start in ((mine_ref, half), (other_ref, 1 - half)):
        chunk = lambda c: ref[c * n:(c + 1) * n, :]
        for u in range(h):
            v = jnp.where(lane < HALF, pick(chunk, u * patch, 0, lane, patch),
                          pick(chunk, (u + h) * patch, HALF, lane, patch))
            out_ref[pl.ds(start * (n * h) + u, n, stride=h), :] = jnp.where(lane % HALF < patch, v, 0.0)


def pack_fit(mine, other, patch, half):
    n = mine.shape[0] // (patch * patch // LANES)
    return pl.pallas_call(
        functools.partial(pack_fit_kernel, patch=patch, half=half),
        out_shape=jax.ShapeDtypeStruct((2 * n * (patch // 2), LANES), F32),
        in_specs=[vmem()] * 2, out_specs=vmem(),
        compiler_params=pltpu.CompilerParams(vmem_limit_bytes=4 * 1024 * 1024),
    )(mine, other)


def render_kernel(feat_ref, g_ref, gt_ref, dirty_ref, res_ref, tay_ref,
                  words_v, list_v, words_s, amps_s, list_s, acc, acct, sems, *,
                  patch, tile, taylor, scales, origin):
    rows = tile + 2 * patch
    S = feat_ref.shape[1]
    h = patch // 2
    c1 = pltpu.make_async_copy(feat_ref.at[pl.ds(3, taylor)], amps_s.at[:, pl.ds(0, S), :], sems.at[0])
    c1.start()
    r0, c0 = origin()
    rr = feat_ref[0].astype(I32) - r0
    cc = feat_ref[1].astype(I32) - c0
    mask = (rr > -patch) & (rr < tile) & (cc > -patch) & (cc < tile)
    base = jnp.where(mask, ((cc + HALF) >> 6) * rows + rr + patch, 0)
    words_v[...] = base + ((cc & (LANES - 1)) << 14) + (feat_ref[2].astype(I32) << 21)
    c2 = pltpu.make_async_copy(words_v, words_s.at[pl.ds(0, S), :], sems.at[1])
    c2.start()
    mb = jnp.where(mask, 1.0, 0.0).astype(BF16)
    i0 = lax.broadcasted_iota(I32, (LANES, LANES), 0)
    i1 = lax.broadcasted_iota(I32, (LANES, LANES), 1)
    upper = jnp.where(i0 < i1, 1.0, 0.0).astype(BF16)
    ones = jnp.ones((LANES, LANES), BF16)
    s0 = lax.broadcasted_iota(I32, (S, S), 0)
    s1 = lax.broadcasted_iota(I32, (S, S), 1)
    below = jnp.where(s1 < s0, 1.0, 0.0).astype(BF16)
    before = jnp.dot(below, mb, preferred_element_type=F32).astype(BF16)
    every = jnp.dot(jnp.ones((8, S), BF16), mb, preferred_element_type=F32).astype(BF16)
    rank = jnp.dot(mb, upper, preferred_element_type=F32) + jnp.dot(before, ones, preferred_element_type=F32)
    total = jnp.dot(every, ones, preferred_element_type=F32)
    list_v[S:S + 8, :] = total.astype(I32)
    rank = jnp.where(mask, rank, -1.0).astype(I32)
    lo, hi = rank & (LANES - 1), rank >> 7
    lane_row = lax.broadcasted_iota(I32, (S, LANES), 1).astype(F32)
    srow = lax.broadcasted_iota(I32, (S, LANES), 0)
    got = None
    for d in range(S):
        hit = hi[d:d + 1, :] == srow
        onehot = jnp.where(lo[d:d + 1, :] == i0, 1.0, 0.0).astype(BF16)
        pair = [jnp.where(hit, lane_row, 0.0), jnp.where(hit, float(d), 0.0)]
        one = lax.dot_general(jnp.concatenate(pair, 0).astype(BF16), onehot, (((1,), (1,)), ((), ())),
                              preferred_element_type=F32)
        got = one if got is None else got + one
    list_v[0:S, :] = got[S:].astype(I32) * LANES + got[:S].astype(I32)
    c3 = pltpu.make_async_copy(list_v, list_s, sems.at[2])
    c3.start()
    for j in range(1, acc.shape[0] // rows - 1):
        acc[pl.ds(j * rows + patch, tile), :] = jnp.zeros((tile, LANES), F32)
        acct[pl.ds(j * rows + patch - h, tile + h), :] = jnp.zeros((tile + h, LANES), F32)
    c1.wait()
    c2.wait()
    c3.wait()
    for t in range(taylor):
        amps_s[t, S, 0] = 0.0
    words_s[S, 0] = 0
    n = list_s[S, 0]
    lane_half = lax.broadcasted_iota(I32, (1, LANES), 1) & (HALF - 1)

    def gen(it, k):
        row, col = it // (LANES // U), (it % (LANES // U)) * U + k
        idx = jnp.where(it * U + k < n, list_s[row, col], S * LANES)
        row, col = idx >> 7, idx & (LANES - 1)
        word = words_s[row, col]
        base, turn, width = word & 16383, (word >> 14) & (LANES - 1), word >> 21
        gb, hb = pl.multiple_of(width * patch, 8), pl.multiple_of(width * h, 8)
        p = q = None
        for t in range(taylor):
            a = amps_s[t, row, col]
            x = a * g_ref[pl.ds(gb + t * scales * patch, patch), :]
            y = a * gt_ref[pl.ds(hb + t * scales * h, h), :]
            p, q = (x, y) if p is None else (p + x, q + y)
        p = p.astype(BF16).astype(F32)
        return pltpu.roll(p, turn, 1), pltpu.roll(q, turn, 1), base, turn & (HALF - 1)

    def put(p, q, base, turn):
        first = lane_half >= turn
        for ref, val, high in ((acc, p, patch), (acct, q, h)):
            here, right = pl.ds(base, high), pl.ds(base + rows, high)
            ref[here, :] = ref[here, :] + jnp.where(first, val, 0.0)
            ref[right, :] = ref[right, :] + jnp.where(first, 0.0, val)

    def step(i, carry):
        for item in [gen(i, k) for k in range(U)]:
            put(*item)
        return carry

    lax.fori_loop(0, (n + U - 1) // U, step, 0)

    left = lax.broadcasted_iota(I32, (tile, LANES), 1) < HALF
    for c in range(tile // LANES):
        j, cols = 2 * c + 1, slice(c * LANES, (c + 1) * LANES)

        def get(ref, jj, top):
            return ref[pl.ds(jj * rows + top, tile), :]

        x, y = get(acc, j, patch), get(acc, j + 1, patch)
        res_ref[0, :, cols] = dirty_ref[0, :, cols] - jnp.where(left, x, y)
        res_ref[1, :, cols] = dirty_ref[1, :, cols] - pltpu.roll(jnp.where(left, y, x), HALF, 1)
        up = jnp.where(left, get(acct, j, patch), get(acct, j + 1, patch))
        low = pltpu.roll(jnp.where(left, get(acct, j + 1, patch - h), get(acct, j, patch - h)), HALF, 1)
        tay_ref[0, :, cols] = up + low


def render(feats, g, gt, dirty, origin, *, patch, taylor, scales):
    tile, S = dirty.shape[1], feats.shape[1]
    rows, tiles = tile + 2 * patch, tile // HALF + 2
    return pl.pallas_call(
        functools.partial(render_kernel, patch=patch, tile=tile, taylor=taylor, scales=scales, origin=origin),
        out_shape=(jax.ShapeDtypeStruct(dirty.shape, F32), jax.ShapeDtypeStruct((1,) + dirty.shape[1:], F32)),
        in_specs=[vmem()] * 4, out_specs=(vmem(),) * 2,
        scratch_shapes=[
            pltpu.VMEM((S, LANES), I32), pltpu.VMEM((S + 8, LANES), I32),
            pltpu.SMEM((S + 1, LANES), I32), pltpu.SMEM((taylor, S + 1, LANES), F32), pltpu.SMEM((S + 8, LANES), I32),
            pltpu.VMEM((tiles * rows, LANES), F32), pltpu.VMEM((tiles * rows, LANES), F32),
            pltpu.SemaphoreType.DMA((3,))],
        compiler_params=pltpu.CompilerParams(vmem_limit_bytes=8 * 1024 * 1024),
    )(feats, g, gt, dirty)


def per_device(dirty, psf, comp_tile, comp_offset, comp_scale, comp_amp, fit_weight):
    bands, tile = dirty.shape[0], dirty.shape[1]
    patch = math.isqrt(psf.shape[2])
    taylor = comp_amp.shape[1]
    scales = psf.shape[1] // taylor
    n_ty, n_tx, n_band = lax.axis_size("ty"), lax.axis_size("tx"), lax.axis_size("band")
    half = lambda: lax.axis_index("ty") % 2
    feats, dirty_parts, psi_parts, planes = prep(
        dirty, psf, comp_tile, comp_offset, comp_scale, comp_amp, fit_weight,
        lambda: lax.axis_index("band"), half, n_tx, n_band)
    lift = 2.0 ** math.floor(math.log2(60000.0 / (bands * 30.0)))

    def sent(parts):
        return [lax.ppermute((parts[s] * lift).astype(jnp.float16), "band", [(i, i ^ s) for i in range(n_band)])
                for s in range(1, n_band)]

    def summed(parts, got):
        total = parts[0]
        for value in got:
            total = total + value.astype(F32) * (1.0 / lift)
        return total

    psi = summed(psi_parts, sent(psi_parts))
    dirty_got = sent(dirty_parts)
    bit = 1
    while bit < n_ty * n_tx:
        other = lax.ppermute(feats, ("ty", "tx"), [(i, i ^ bit) for i in range(n_ty * n_tx)])
        feats = jnp.concatenate([feats, other], 1)
        bit *= 2
    psi_other = lax.ppermute(psi, "ty", [(i, i ^ 1) for i in range(n_ty)])
    residual, model_fit = render(
        feats, pack(planes, patch), pack_fit(psi, psi_other, patch, half), dirty,
        lambda: (lax.axis_index("ty") * tile, lax.axis_index("tx") * tile),
        patch=patch, taylor=taylor, scales=scales)
    return residual, summed(dirty_parts, dirty_got)[None] - model_fit


def solution(mesh):
    return jax.shard_map(
        per_device,
        mesh=mesh,
        in_specs=(
            P("band", "ty", "tx"),
            P("band", None, None),
            P(("ty", "tx"), None),
            P(("ty", "tx"), None),
            P(("ty", "tx")),
            P(("ty", "tx"), None),
            P("band", None),
        ),
        out_specs=(P("band", "ty", "tx"), P("band", "ty", "tx")),
        check_vma=False,
    )
```

time: 122 us -> 27.1 us (0.22)
  waiting for transfers between devices: 41.7 us -> 5.11 us
  matrix products: 27.9 us -> 0 us
  local copies, waits for them, and re-layouts: 18.2 us -> 0.01 us
  between operations: 14.2 us -> 0.77 us
  Pallas kernels: 0 us -> 6.58 us
  other arithmetic: 6.25 us -> 1.01 us
    reduce_scatter x1 -> x0, waiting for transfers between devices: 32.3 us -> none  [per_device(): lax.psum_scatter(jnp.einsum('bt,byx->tyx', fit_weight, residual, precisio...]
    dot_general x33 -> x0, matrix products: 27.9 us -> none  [the longest x16 20.4 us: step(): jnp.einsum('hk,bkw->bhw', row_table, placed, preferred_element_type=jnp.f...]
    ppermute x2 -> x10, starting transfers between devices: 3.91 us -> 13.4 us  [the longest x6 8.7 us: sent(): lax.ppermute((parts[s] * lift).astype(jnp.float16), 'band', [(i, i ^ s) f...]
    reshape x17 -> x0, local copies, waits for them, and re-layouts: 9.03 us -> none  [the longest x16 8.79 us: step(): patch_four = patch_blk.reshape(block, bands_here, PATCH, PATCH)]
    all_to_all x2 -> x0, starting transfers between devices: 8.48 us -> none  [the longest x1 5.17 us: per_device(): lax.all_to_all(packed, ('ty', 'tx'), split_axis=0, concat_axis=0, tiled=T...]
    pallas_call x0 -> x4, Pallas kernels: none -> 6.58 us  [the longest x1 4.46 us: render(): pl.pallas_call(functools.partial(render_kernel, patch=patch, tile=tile, t...]
    all_to_all x2 -> x0, waiting for transfers between devices: 6.43 us -> none  [the longest x1 3.4 us: per_device(): lax.all_to_all(amps_send, ('ty', 'tx'), split_axis=0, concat_axis=0, tile...]
    reduce_sum x4 -> x0, other arithmetic: 3.39 us -> none  [the longest x3 2.49 us: pick_rows(): jnp.sum(jnp.where(onehot[:, :, None], values[None, :, :], jnp.zeros((), v...]
  transfers between devices with their start and end apart: 5 -> 10, of which waited for: 5 -> 2; matrix products, arithmetic and copies ran while one was open for 2% -> 1% of each run, Pallas kernels for 0% -> 19%
where the time goes in v2:
time: 27.1 us; the launch traced here: 26.9 us
  starting transfers between devices  13.4 us (49%)
  Pallas kernels  6.58 us (24%)
  waiting for transfers between devices  5.11 us (19%)
  other arithmetic  1.01 us (4%)
  between operations  0.77 us (3%)
    ppermute x6, starting transfers between devices, sent(): lax.ppermute((parts[s] * lift).astype(jnp.float16), 'band', [(i, i ^ s) f...  8.7 us
    ppermute x3, starting transfers between devices, per_device(): lax.ppermute(feats, ('ty', 'tx'), [(i, i ^ bit) for i in range(n_ty * n_t...  4.66 us
    pallas_call x1, Pallas kernels, render(): pl.pallas_call(functools.partial(render_kernel, patch=patch, tile=tile, t...  4.46 us
    ppermute x6, waiting for transfers between devices, sent(): lax.ppermute((parts[s] * lift).astype(jnp.float16), 'band', [(i, i ^ s) f...  3.03 us
    ppermute x3, waiting for transfers between devices, per_device(): lax.ppermute(feats, ('ty', 'tx'), [(i, i ^ bit) for i in range(n_ty * n_t...  2.08 us
    pallas_call x1, Pallas kernels, prep(): pl.pallas_call(functools.partial(prep_kernel, me=me, half=half, n_tx=n_tx...  1.51 us
    sub x1, other arithmetic, per_device(): return (residual, summed(dirty_parts, dirty_got)[None] - model_fit)  0.81 us
  transfers between devices with their start and end apart: 10, of which 2 were waited for; matrix products, arithmetic and copies ran while one was open for 1% of the time, Pallas kernels for 19%

profile of v2, /device:TPU:0, one launch (start us, length us, event | category | flops | bytes accessed | tf_op | source)
XLA Modules:
  0.0 26.9 jit_solution(3889779066594556194)
XLA Ops:
  0.6 1.5 %shard_map.86 = (f32[7,1,128]{2,1,0:T(1,128)S(1)}, f32[4,256,256]{2,1,0:T(8,128)S(1)}, f32[4,180,128]{2,1,0:T(8,128)S(1)}, f32[2,20,2304]{2,1,0:T(8,128)S(1)}) custom-call(f32[2,4]{1,0:T(2,128)} %w_hbm.1, s32[1,128]{1,0:T(1,128)} %bitcast.36, s32[2,128]{1,0:T(2,128)} %bitcast.35, s32[1,128]{1,0:T(1,128)} %bitcast.37, f32[4,128]{1,0:T(4,128)} %bitcast.34, ...), custom_call_target="tpu_custom_call" | custom-call | tf_op jit(solution)/shard_map/pallas_call | solution.py:79
  2.1 3.0 %collective-permute-start = (f32[7,1,128]{2,1,0:T(1,128)S(1)}, f32[7,1,128]{2,1,0:T(1,128)S(1)}, u32[]{:S(2)}, u32[]{:S(2)}) collective-permute-start(f32[7,1,128]{2,1,0:T(1,128)S(1)} %get-tuple-element.8), channel_id=1, source_target_pairs={{0,1},{1,0},{2,3},{3,2},{4,5},{5,4},{6,7},{7,6},{8,9},{9,8},{10,11... | collective-permute-start | bytes 10760 | tf_op jit(solution)/shard_map/ppermute | solution.py:292
  5.2 1.6 %collective-permute-start.3 = (f16[180,128]{1,0:T(8,128)(2,1)S(1)}, f16[180,128]{1,0:T(8,128)(2,1)S(1)}, u32[]{:S(2)}, u32[]{:S(2)}) collective-permute-start(f16[180,128]{1,0:T(8,128)(2,1)S(1)} %get-tuple-element.17), channel_id=1, source_target_pairs={{0,8},{8,0},{16,24},{24,16},{1,9},{9,1},{17,25},{25,17},{2,10},{10... | collective-permute-start | bytes 138248 | tf_op jit(solution)/shard_map/ppermute | solution.py:279
  6.8 2.5 %collective-permute-start.5 = (f16[180,128]{1,0:T(8,128)(2,1)S(1)}, f16[180,128]{1,0:T(8,128)(2,1)S(1)}, u32[]{:S(2)}, u32[]{:S(2)}) collective-permute-start(f16[180,128]{1,0:T(8,128)(2,1)S(1)} %get-tuple-element.18), channel_id=1, source_target_pairs={{0,24},{8,16},{16,8},{24,0},{1,25},{9,17},{17,9},{25,1},{2,26},{10... | collective-permute-start | bytes 138248 | tf_op jit(solution)/shard_map/ppermute | solution.py:279
  9.3 0.1 collective-permute-start.4
  9.4 0.0 collective-permute-done
  9.4 0.1 collective-permute-start.1
  9.5 0.1 fusion.2
  9.6 1.9 %collective-permute-start.7 = (f16[256,256]{1,0:T(8,128)(2,1)S(1)}, f16[256,256]{1,0:T(8,128)(2,1)S(1)}, u32[]{:S(2)}, u32[]{:S(2)}) collective-permute-start(f16[256,256]{1,0:T(8,128)(2,1)S(1)} %get-tuple-element.14), channel_id=1, source_target_pairs={{0,8},{8,0},{16,24},{24,16},{1,9},{9,1},{17,25},{25,17},{2,10},{10... | collective-permute-start | bytes 393224 | tf_op jit(solution)/shard_map/ppermute | solution.py:279
  11.5 0.4 %shard_map.87.g_ref = f32[960,128]{1,0:T(8,128)S(1)} custom-call(f32[2,20,2304]{2,1,0:T(8,128)S(1)} %get-tuple-element.9.psf_ref), custom_call_target="tpu_custom_call" | custom-call | tf_op jit(solution)/shard_map/pallas_call | solution.py:118
  11.9 0.0 copy-start
  11.9 0.0 collective-permute-done.1
  11.9 2.5 %collective-permute-start.9 = (f16[256,256]{1,0:T(8,128)(2,1)S(1)}, f16[256,256]{1,0:T(8,128)(2,1)S(1)}, u32[]{:S(2)}, u32[]{:S(2)}) collective-permute-start(f16[256,256]{1,0:T(8,128)(2,1)S(1)} %get-tuple-element.15), channel_id=1, source_target_pairs={{0,24},{8,16},{16,8},{24,0},{1,25},{9,17},{17,9},{25,1},{2,26},{10... | collective-permute-start | bytes 393224 | tf_op jit(solution)/shard_map/ppermute | solution.py:279
  14.4 0.0 collective-permute-done.3
  14.4 0.1 collective-permute-start.8
  14.5 0.0 collective-permute-done.5
  14.5 1.6 %collective-permute-start.2 = (f32[7,4,128]{2,1,0:T(4,128)S(1)}, f32[7,4,128]{2,1,0:T(4,128)S(1)}, u32[]{:S(2)}, u32[]{:S(2)}) collective-permute-start(f32[7,4,128]{2,1,0:T(4,128)S(1)} %pad_maximum_fusion.1), channel_id=1, source_target_pairs={{0,4},{1,5},{2,6},{3,7},{4,0},{5,1},{6,2},{7,3},{8,12},{9,13},{10,... | collective-permute-start | bytes 43016 | tf_op jit(solution)/shard_map/ppermute | solution.py:292
  16.1 0.0 collective-permute-done.4
  16.2 0.1 collective-permute-start.6
  16.2 2.1 %collective-permute-done.2 = f32[7,4,128]{2,1,0:T(4,128)S(1)} collective-permute-done((f32[7,4,128]{2,1,0:T(4,128)S(1)}, f32[7,4,128]{2,1,0:T(4,128)S(1)}, u32[]{:S(2)}, u32[]{:S(2)}) %collective-permute-start.2) | collective-permute-done | bytes 14368 | tf_op jit(solution)/shard_map/ppermute | solution.py:292
  18.3 0.0 collective-permute-done.6.other_ref
  18.3 0.2 shard_map.88.gt_ref
  18.6 0.0 copy-done
  18.6 4.5 %shard_map.89 = (f32[2,256,256]{2,1,0:T(8,128)}, f32[1,256,256]{2,1,0:T(8,128)S(1)}) custom-call(f32[7,8,128]{2,1,0:T(8,128)S(1)} %pad_maximum_fusion.feat_ref, f32[960,128]{1,0:T(8,128)S(1)} %shard_map.87.g_ref, f32[480,128]{1,0:T(8,128)S(1)} %shard_map.88.gt_ref, f32[2,256,256]{2,1,0:T(8,128)S(1)} %copy-done), custom_call_target="tpu_custom_call" | custom-call | tf_op jit(solution)/shard_map/pallas_call | solution.py:253
  23.1 0.0 collective-permute-done.7
  23.1 0.0 collective-permute-done.9
  23.1 3.0 %collective-permute-done.8 = f16[256,256]{1,0:T(8,128)(2,1)S(1)} collective-permute-done((f16[256,256]{1,0:T(8,128)(2,1)S(1)}, f16[256,256]{1,0:T(8,128)(2,1)S(1)}, u32[]{:S(2)}, u32[]{:S(2)}) %collective-permute-start.8) | collective-permute-done | bytes 131104 | tf_op jit(solution)/shard_map/ppermute | solution.py:279
  26.1 0.8 %bitcast_subtract_fusion = f32[1,256,256]{2,1,0:T(8,128)} fusion(f32[1,256,256]{2,1,0:T(8,128)S(1)} %get-tuple-element.13, f16[256,256]{1,0:T(8,128)(2,1)S(1)} %collective-permute-done.9, f16[256,256]{1,0:T(8,128)(2,1)S(1)} %collective-permute-done.8, f16[256,256]{1,0:T(8,128)(2,1)S(1)} %collective-permute-done.7, f32[4,256,256]{2,1,0:T(8,128)S(1)} %get-tuple-element.12), kind=kLoop, calls=%fused_computation | loop fusion | flops 655360 | bytes 1179648 | tf_op jit(solution)/shard_map/sub | solution.py:300
  (5 shorter events, 0.1 us)
Async XLA Ops:
  2.1 7.3 %collective-permute-start = (f32[7,1,128]{2,1,0:T(1,128)S(1)}, f32[7,1,128]{2,1,0:T(1,128)S(1)}, u32[]{:S(2)}, u32[]{:S(2)}) collective-permute-start(f32[7,1,128]{2,1,0:T(1,128)S(1)} %get-tuple-element.8), channel_id=1, source_target_pairs={{0,1},{1,0},{2,3},{3,2},{4,5},{5,4},{6,7},{7,6},{8,9},{9,8},{10,11... | collective-permute-start | bytes 10760 | tf_op jit(solution)/shard_map/ppermute | solution.py:292
  5.2 9.2 %collective-permute-start.3 = (f16[180,128]{1,0:T(8,128)(2,1)S(1)}, f16[180,128]{1,0:T(8,128)(2,1)S(1)}, u32[]{:S(2)}, u32[]{:S(2)}) collective-permute-start(f16[180,128]{1,0:T(8,128)(2,1)S(1)} %get-tuple-element.17), channel_id=1, source_target_pairs={{0,8},{8,0},{16,24},{24,16},{1,9},{9,1},{17,25},{25,17},{2,10},{10... | collective-permute-start | bytes 138248 | tf_op jit(solution)/shard_map/ppermute | solution.py:279
  6.8 7.7 %collective-permute-start.5 = (f16[180,128]{1,0:T(8,128)(2,1)S(1)}, f16[180,128]{1,0:T(8,128)(2,1)S(1)}, u32[]{:S(2)}, u32[]{:S(2)}) collective-permute-start(f16[180,128]{1,0:T(8,128)(2,1)S(1)} %get-tuple-element.18), channel_id=1, source_target_pairs={{0,24},{8,16},{16,8},{24,0},{1,25},{9,17},{17,9},{25,1},{2,26},{10... | collective-permute-start | bytes 138248 | tf_op jit(solution)/shard_map/ppermute | solution.py:279
  9.3 6.8 %collective-permute-start.4 = (f16[180,128]{1,0:T(8,128)(2,1)S(1)}, f16[180,128]{1,0:T(8,128)(2,1)S(1)}, u32[]{:S(2)}, u32[]{:S(2)}) collective-permute-start(f16[180,128]{1,0:T(8,128)(2,1)S(1)} %get-tuple-element.19), channel_id=1, source_target_pairs={{0,16},{8,24},{16,0},{24,8},{1,17},{9,25},{17,1},{25,9},{2,18},{10... | collective-permute-start | bytes 138248 | tf_op jit(solution)/shard_map/ppermute | solution.py:279
  9.4 2.4 %collective-permute-start.1 = (f32[7,2,128]{2,1,0:T(2,128)S(1)}, f32[7,2,128]{2,1,0:T(2,128)S(1)}, u32[]{:S(2)}, u32[]{:S(2)}) collective-permute-start(f32[7,2,128]{2,1,0:T(2,128)S(1)} %pad_maximum_fusion.2), channel_id=1, source_target_pairs={{0,2},{1,3},{2,0},{3,1},{4,6},{5,7},{6,4},{7,5},{8,10},{9,11},{10,... | collective-permute-start | bytes 21512 | tf_op jit(solution)/shard_map/ppermute | solution.py:292
  9.6 13.5 %collective-permute-start.7 = (f16[256,256]{1,0:T(8,128)(2,1)S(1)}, f16[256,256]{1,0:T(8,128)(2,1)S(1)}, u32[]{:S(2)}, u32[]{:S(2)}) collective-permute-start(f16[256,256]{1,0:T(8,128)(2,1)S(1)} %get-tuple-element.14), channel_id=1, source_target_pairs={{0,8},{8,0},{16,24},{24,16},{1,9},{9,1},{17,25},{25,17},{2,10},{10... | collective-permute-start | bytes 393224 | tf_op jit(solution)/shard_map/ppermute | solution.py:279
  11.9 6.7 %copy-start = (f32[2,256,256]{2,1,0:T(8,128)S(1)}, f32[2,256,256]{2,1,0:T(8,128)}, u32[]{:S(2)}) copy-start(f32[2,256,256]{2,1,0:T(8,128)} %dirty_ref.1) | copy-start | bytes 1572868
  11.9 11.2 %collective-permute-start.9 = (f16[256,256]{1,0:T(8,128)(2,1)S(1)}, f16[256,256]{1,0:T(8,128)(2,1)S(1)}, u32[]{:S(2)}, u32[]{:S(2)}) collective-permute-start(f16[256,256]{1,0:T(8,128)(2,1)S(1)} %get-tuple-element.15), channel_id=1, source_target_pairs={{0,24},{8,16},{16,8},{24,0},{1,25},{9,17},{17,9},{25,1},{2,26},{10... | collective-permute-start | bytes 393224 | tf_op jit(solution)/shard_map/ppermute | solution.py:279
  14.4 11.7 %collective-permute-start.8 = (f16[256,256]{1,0:T(8,128)(2,1)S(1)}, f16[256,256]{1,0:T(8,128)(2,1)S(1)}, u32[]{:S(2)}, u32[]{:S(2)}) collective-permute-start(f16[256,256]{1,0:T(8,128)(2,1)S(1)} %get-tuple-element.16), channel_id=1, source_target_pairs={{0,16},{8,24},{16,0},{24,8},{1,17},{9,25},{17,1},{25,9},{2,18},{10... | collective-permute-start | bytes 393224 | tf_op jit(solution)/shard_map/ppermute | solution.py:279
  14.5 3.8 %collective-permute-start.2 = (f32[7,4,128]{2,1,0:T(4,128)S(1)}, f32[7,4,128]{2,1,0:T(4,128)S(1)}, u32[]{:S(2)}, u32[]{:S(2)}) collective-permute-start(f32[7,4,128]{2,1,0:T(4,128)S(1)} %pad_maximum_fusion.1), channel_id=1, source_target_pairs={{0,4},{1,5},{2,6},{3,7},{4,0},{5,1},{6,2},{7,3},{8,12},{9,13},{10,... | collective-permute-start | bytes 43016 | tf_op jit(solution)/shard_map/ppermute | solution.py:292
  16.2 2.2 %collective-permute-start.6 = (f32[180,128]{1,0:T(8,128)S(1)}, f32[180,128]{1,0:T(8,128)S(1)}, u32[]{:S(2)}, u32[]{:S(2)}) collective-permute-start(f32[180,128]{1,0:T(8,128)S(1)} %fusion.6.mine_ref), channel_id=1, source_target_pairs={{0,2},{2,0},{4,6},{6,4},{1,3},{3,1},{5,7},{7,5},{8,10},{10,8},{12,... | collective-permute-start | bytes 276488 | tf_op jit(solution)/shard_map/ppermute | solution.py:295
